TPU v7x, 256 devices: a whole 4x4x8 slice. The times are simulated.
256 devices in a mesh: clip: 16 (over x, y), tm: 16 (over z, core).
Axes of the slice: x: 4, y: 4, z: 8, core: 2. Of those that a mesh axis runs over, the one named last changes fastest.
Arguments:
- x_inner: bfloat16 [256, 192, 2048], P(('clip', 'tm')), parts along dimension 0, may hold values from -6 to 6
- bc_inputs: bfloat16 [256, 192, 256], P(('clip', 'tm')), parts along dimension 0, may hold values from -2 to 2
- step_raw: bfloat16 [256, 192, 64], P(('clip', 'tm')), parts along dimension 0, may hold values from -5 to 5
- decay_rate: float32 [2, 32], replicated, may hold values from 0.002 to 0.3
- skip_gain: float32 [32], replicated, may hold values from 0.1 to 1.9
- w_out: bfloat16 [2048, 1024], P('tm'), may hold values from -0.125 to 0.125
- grad_out: bfloat16 [256, 192, 1024], P(('clip', 'tm')), parts along dimension 0, may hold values from -6 to 6
Outputs:
- mixed_out: bfloat16 [256, 192, 1024], P(('clip', 'tm')), parts along dimension 0
- grad_inner: bfloat16 [256, 192, 2048], P(('clip', 'tm')), parts along dimension 0
- grad_bc: bfloat16 [256, 192, 256], P(('clip', 'tm')), parts along dimension 0
- grad_step: bfloat16 [256, 192, 64], P(('clip', 'tm')), parts along dimension 0
- grad_w_out: float32 [32768, 1024], P(('clip', 'tm')), parts along dimension 0
There are 16 independent parts, one for each index of `clip`. A program takes and returns all parts, laid end to end along the dimension named above; an argument that names none is the same for every part. Nothing has to cross between parts.
All inputs are finite; a program needn't handle non-finite values.
Results may differ from a plain program's by a relative error of at most 0.022.
Values may be sent and summed in bfloat16 or wider, within the bound.
No kernel may reach another device: no remote copies, remote signals or barrier semaphores. Data moves between devices by JAX's collectives and lax.ppermute only.
A program may use at most 128 MiB of HBM per device.

v0:
```python
import math

import jax
import jax.numpy as jnp
from jax import lax
from jax.sharding import PartitionSpec as P

HIGH = lax.Precision.HIGHEST


def block_scan(heads_in, b_rows, c_rows, step_size, decay_rates, block_len):
    length, nheads, head_dim = heads_in.shape
    block_count = length // block_len
    state_size = b_rows.shape[-1]
    x_blocks = heads_in.reshape(block_count, block_len, nheads, head_dim)
    b_blocks = b_rows.reshape(block_count, block_len, state_size)
    c_blocks = c_rows.reshape(block_count, block_len, state_size)
    s_blocks = step_size.reshape(block_count, block_len, nheads)
    log_cum = jnp.cumsum(-s_blocks * decay_rates, axis=1)
    log_gaps = log_cum[:, :, None, :] - log_cum[:, None, :, :]
    lower_mask = jnp.arange(block_len)[:, None] >= jnp.arange(block_len)[None, :]
    decay_mat = jnp.exp(jnp.where(lower_mask[None, :, :, None], log_gaps, -jnp.inf))
    gram_mat = jnp.einsum("kin,kjn->kij", c_blocks, b_blocks, precision=HIGH)
    weights = gram_mat[:, :, :, None] * decay_mat * s_blocks[:, None, :, :]
    inside = jnp.einsum("kijh,kjhd->kihd", weights, x_blocks, precision=HIGH)
    log_last = log_cum[:, -1, :]
    tail_weight = jnp.exp(log_last[:, None, :] - log_cum) * s_blocks
    states = jnp.einsum("kjh,kjhd,kjn->khdn", tail_weight, x_blocks, b_blocks, precision=HIGH)

    def advance(state_carry, inputs):
        log_end, added_state = inputs
        return (jnp.exp(log_end)[:, None, None] * state_carry + added_state, state_carry)

    final_state, entering = lax.scan(
        advance, jnp.zeros(states.shape[1:], states.dtype), (log_last, states)
    )
    outside = (
        jnp.einsum("kin,khdn->kihd", c_blocks, entering, precision=HIGH)
        * jnp.exp(log_cum)[:, :, :, None]
    )
    return (inside + outside).reshape(length, nheads, head_dim)


def whole_scan(heads_in, b_rows, c_rows, step_size, decay_rates):
    length = heads_in.shape[0]
    log_cum = jnp.cumsum(-step_size * decay_rates, axis=0)
    log_gaps = log_cum[:, None, :] - log_cum[None, :, :]
    lower_mask = jnp.arange(length)[:, None] >= jnp.arange(length)[None, :]
    decay_mat = jnp.exp(jnp.where(lower_mask[:, :, None], log_gaps, -jnp.inf))
    gram_mat = jnp.einsum("in,jn->ij", c_rows, b_rows, precision=HIGH)
    weights = gram_mat[:, :, None] * decay_mat * step_size[None, :, :]
    return jnp.einsum("ijh,jhd->ihd", weights, heads_in, precision=HIGH)


def spatial_mix(x_vals, b_vals, c_vals, raw_vals, decay_rates):
    frames, patches, inner_width = x_vals.shape
    nheads = decay_rates.shape[0]
    step_size = jax.nn.softplus(raw_vals)
    heads_in = x_vals.reshape(frames, patches, nheads, inner_width // nheads)
    block_len = math.gcd(patches, 64)

    def one_frame(x_one, b_one, c_one, s_one):
        return block_scan(x_one, b_one, c_one, s_one, decay_rates, block_len)

    result = jax.vmap(one_frame)(heads_in, b_vals, c_vals, step_size)
    return result.reshape(frames, patches, inner_width)


def temporal_mix(x_vals, b_vals, c_vals, raw_vals, decay_rates, skip_gain):
    frames, patches, inner_width = x_vals.shape
    nheads = decay_rates.shape[0]
    step_size = jax.nn.softplus(raw_vals)
    heads_in = x_vals.reshape(frames, patches, nheads, inner_width // nheads)

    def one_patch(x_one, b_one, c_one, s_one):
        return whole_scan(x_one, b_one, c_one, s_one, decay_rates)

    result = jax.vmap(one_patch, in_axes=1, out_axes=1)(heads_in, b_vals, c_vals, step_size)
    result = result + skip_gain[None, None, :, None] * heads_in
    return result.reshape(frames, patches, inner_width)


def on_device(x_inner, bc_inputs, step_raw, decay_rate, skip_gain, w_out, grad_out):
    state_size = bc_inputs.shape[-1] // 4
    nheads = skip_gain.shape[0]
    local_frames, patches, inner_width = x_inner.shape
    model_width = w_out.shape[1]

    def spatial_fn(x_vals, b_vals, c_vals, raw_vals):
        return spatial_mix(x_vals, b_vals, c_vals, raw_vals, decay_rate[0])

    def temporal_fn(x_vals, b_vals, c_vals, raw_vals):
        return temporal_mix(x_vals, b_vals, c_vals, raw_vals, decay_rate[1], skip_gain)

    spatial_out, spatial_back = jax.vjp(
        spatial_fn,
        x_inner.astype(jnp.float32),
        bc_inputs[:, :, :state_size].astype(jnp.float32),
        bc_inputs[:, :, state_size : 2 * state_size].astype(jnp.float32),
        step_raw[:, :, :nheads].astype(jnp.float32),
    )
    spatial_bf = spatial_out.astype(jnp.bfloat16)
    weight_full = lax.all_gather(w_out, "tm", axis=0, tiled=True)
    carried = lax.dot_general(
        grad_out.reshape(-1, model_width),
        weight_full,
        (((1,), (1,)), ((), ())),
        preferred_element_type=jnp.float32,
    )
    carried = carried.astype(jnp.bfloat16).reshape(local_frames, patches, inner_width)
    spatial_here, temporal_bc, temporal_raw, carried_here = (
        lax.all_to_all(spatial_bf, "tm", split_axis=1, concat_axis=0, tiled=True),
        lax.all_to_all(
            bc_inputs[:, :, 2 * state_size :], "tm", split_axis=1, concat_axis=0, tiled=True
        ),
        lax.all_to_all(step_raw[:, :, nheads:], "tm", split_axis=1, concat_axis=0, tiled=True),
        lax.all_to_all(carried, "tm", split_axis=1, concat_axis=0, tiled=True),
    )
    mixed, temporal_back = jax.vjp(
        temporal_fn,
        spatial_here.astype(jnp.float32),
        temporal_bc[:, :, :state_size].astype(jnp.float32),
        temporal_bc[:, :, state_size:].astype(jnp.float32),
        temporal_raw.astype(jnp.float32),
    )
    mixed_bf = mixed.astype(jnp.bfloat16)
    grad_spatial32, grad_bt, grad_ct, grad_raw_t = temporal_back(carried_here.astype(jnp.float32))
    back_bc = jnp.concatenate([grad_bt, grad_ct], axis=-1).astype(jnp.bfloat16)
    first_back, grad_spatial, bc_back, raw_back = (
        lax.all_to_all(mixed_bf, "tm", split_axis=0, concat_axis=1, tiled=True),
        lax.all_to_all(
            grad_spatial32.astype(jnp.bfloat16), "tm", split_axis=0, concat_axis=1, tiled=True
        ),
        lax.all_to_all(back_bc, "tm", split_axis=0, concat_axis=1, tiled=True),
        lax.all_to_all(
            grad_raw_t.astype(jnp.bfloat16), "tm", split_axis=0, concat_axis=1, tiled=True
        ),
    )
    mixed_rows = first_back.reshape(-1, inner_width)
    grad_rows = grad_out.reshape(-1, model_width)
    mixed_out = jnp.dot(mixed_rows, weight_full, preferred_element_type=jnp.float32)
    mixed_out = mixed_out.astype(jnp.bfloat16).reshape(local_frames, patches, model_width)
    grad_w_out = lax.psum_scatter(
        lax.dot_general(
            mixed_rows, grad_rows, (((0,), (0,)), ((), ())), preferred_element_type=jnp.float32
        ).astype(jnp.bfloat16),
        "tm",
        scatter_dimension=0,
        tiled=True,
    ).astype(jnp.float32)
    grad_x32, grad_bs, grad_cs, grad_raw_s = spatial_back(grad_spatial.astype(jnp.float32))
    grad_bc = jnp.concatenate(
        [grad_bs.astype(jnp.bfloat16), grad_cs.astype(jnp.bfloat16), bc_back], axis=-1
    )
    grad_step = jnp.concatenate([grad_raw_s.astype(jnp.bfloat16), raw_back], axis=-1)
    return (mixed_out, grad_x32.astype(jnp.bfloat16), grad_bc, grad_step, grad_w_out)


def solution(mesh):
    in_specs = (
        P(("clip", "tm"), None, None),
        P(("clip", "tm"), None, None),
        P(("clip", "tm"), None, None),
        P(),
        P(),
        P("tm", None),
        P(("clip", "tm"), None, None),
    )
    out_specs = (
        P(("clip", "tm"), None, None),
        P(("clip", "tm"), None, None),
        P(("clip", "tm"), None, None),
        P(("clip", "tm"), None, None),
        P(("clip", "tm"), None),
    )
    return jax.shard_map(
        on_device, mesh=mesh, in_specs=in_specs, out_specs=out_specs, check_vma=False
    )
```

profile of v0, /device:TPU:1, one launch (start us, length us, event | category | flops | bytes accessed | tf_op | source)
XLA Modules:
  0.0 368.9 jit_solution(15916419813369811506)
XLA Ops:
  10.9 10.0 %all-to-all-start.2 = ((bf16[16,2,192]{2,1,0:T(2,128)(2,1)}), bf16[16,2,192]{2,1,0:T(2,128)(2,1)S(1)}, u32[]{:S(2)}, u32[]{:S(2)}) async-start(bf16[16,2,192]{2,1,0:T(2,128)(2,1)} %reshape.482), calls=%async_computation.2 | async-start | bytes 32768 | tf_op jit(solution)/shard_map/all_to_all | solution.py:116
  51.6 7.9 %all-to-all-start.1 = ((bf16[16,2,768]{2,1,0:T(2,128)(2,1)}), bf16[16,2,768]{2,1,0:T(2,128)(2,1)S(1)}, u32[]{:S(2)}, u32[]{:S(2)}) async-start(bf16[16,2,768]{2,1,0:T(2,128)(2,1)} %reshape.484), calls=%async_computation.1 | async-start | bytes 98304 | tf_op jit(solution)/shard_map/all_to_all | solution.py:113
  64.5 6.1 %reduce.29 = bf16[192,2048]{1,0:T(8,128)(2,1)} reduce(bf16[192,1,2048]{2,1,0:T(2,128)(2,1)S(1)} %bitcast.286, bf16[]{:T(256)} %broadcast.164), dimensions={1}, to_apply=%bitcast.268.reduce_sub_computation | reduce | bytes 1572866
  73.8 7.5 %all-to-all-start.4 = ((bf16[16,2,12288]{2,1,0:T(2,128)(2,1)}), bf16[16,2,12288]{2,1,0:T(2,128)(2,1)}, u32[]{:S(2)}, u32[]{:S(2)}) async-start(bf16[16,2,12288]{2,1,0:T(2,128)(2,1)} %reshape.486), calls=%async_computation.4 | async-start | bytes 1572864 | tf_op jit(solution)/shard_map/all_to_all | solution.py:117
  84.3 19.6 %all-to-all-done.4 = bf16[16,2,12288]{2,1,0:T(2,128)(2,1)} async-done(((bf16[16,2,12288]{2,1,0:T(2,128)(2,1)}), bf16[16,2,12288]{2,1,0:T(2,128)(2,1)}, u32[]{:S(2)}, u32[]{:S(2)}) %all-to-all-start.4) | async-done | bytes 786464 | tf_op jit(solution)/shard_map/all_to_all | solution.py:117
  108.3 5.4 %bitcast_reduce_fusion.1 = bf16[192,2048]{1,0:T(8,128)(2,1)} fusion(bf16[192,1,2048]{2,1,0:T(2,128)(2,1)S(1)} %reshape.487), kind=kLoop, calls=%fused_computation.191 | loop fusion | bytes 1572864 | tf_op jit(solution)/shard_map/all_to_all | solution.py:117
  117.8 5.1 %fusion.13 = bf16[16,12,32,64]{3,0,2,1:T(8,128)(2,1)S(1)} fusion(f32[32]{0:T(128)S(1)} %copy-done.72, f32[12,16,32]{1,2,0:T(8,128)S(1)} %copy.232, f32[12,16,32]{1,2,0:T(8,128)S(1)} %copy.230, f32[12,16,16]{2,1,0:T(8,128)S(1)} %fusion.121, pred[16,16]{1,0:T(8,128)(4,1)S(1)} %iota_compare_fusion.1, bf16[16,12,32,64]{3,2,1,0:T(8,128)(2,1)S(1)} %all_to_all.30), kind=kOutput, calls=%fused_computation.32 | convolution fusion | flops 77463552 | bytes 1634688 | tf_op jit(solution)/shard_map/transpose(jvp(vmap(ijh,jhd->ihd)))/dot_general | solution.py:52
  125.5 4.6 %all-to-all-start.5 = ((bf16[16,12,2048]{2,1,0:T(8,128)(2,1)}), bf16[16,12,2048]{2,1,0:T(8,128)(2,1)}, u32[]{:S(2)}, u32[]{:S(2)}) async-start(bf16[16,12,2048]{2,1,0:T(8,128)(2,1)} %reshape.471), calls=%async_computation.5 | async-start | bytes 2097152 | tf_op jit(solution)/shard_map/all_to_all | solution.py:131
  132.2 9.2 %while.36 = (s32[]{:T(128)}, f32[1,32,64,64]{3,2,1,0:T(8,128)S(1)}, f32[3,1,32,64,64]{4,3,2,1,0:T(8,128)}, f32[3,1,32]{2,1,0:T(1,128)S(1)}, f32[3,1,32,1,1]{2,4,...) while((s32[]{:T(128)}, f32[1,32,64,64]{3,2,1,0:T(8,128)S(1)}, ...), condition=%wide.region_2.3_spmd.clone, body=%wide.region_1.2_spmd.clone.sunk | while | flops 524291 | bytes 3148160 | solution.py:34
  141.4 15.7 %all-to-all-done.5 = bf16[16,12,2048]{2,1,0:T(8,128)(2,1)} async-done(((bf16[16,12,2048]{2,1,0:T(8,128)(2,1)}), bf16[16,12,2048]{2,1,0:T(8,128)(2,1)}, u32[]{:S(2)}, u32[]{:S(2)}) %all-to-all-start.5) | async-done | bytes 786464 | tf_op jit(solution)/shard_map/all_to_all | solution.py:131
  160.9 8.3 %fusion.15 = (f32[3,64,32]{1,2,0:T(8,128)}, f32[3,32,64,64]{2,3,1,0:T(8,128)S(1)}) fusion(f32[3,64,32,64]{3,2,1,0:T(8,128)} %reshape.462, bf16[3,64,64,1]{2,1,3,0:T(8,128)(2,1)} %bitcast.292, f32[3,1,32,64,64]{4,3,2,1,0:T(8,128)S(1)} %copy-done.2), kind=kOutput, calls=%fused_computation.37 | convolution fusion | flops 302770176 | bytes 4767744 | tf_op jit(solution)/shard_map/jvp(vmap(kin,khdn->kihd))/dot_general | solution.py:38
  175.8 5.2 %reduce.30 = bf16[192,2048]{1,0:T(8,128)(2,1)S(1)} reduce(bf16[192,1,2048]{2,1,0:T(2,128)(2,1)S(1)} %bitcast.285, bf16[]{:T(256)} %broadcast.164), dimensions={1}, to_apply=%bitcast.235.reduce_sub_computation | reduce | bytes 1572866
  181.8 26.4 %all_to_all.84 = bf16[16,2,12288]{2,1,0:T(2,128)(2,1)S(1)} all-to-all(bf16[16,2,12288]{2,1,0:T(2,128)(2,1)S(1)} %reshape.488), channel_id=1, replica_groups=mesh['clip'=16,'tm'=16] {'tm'}, dimensions={0} | all-to-all | bytes 1572864 | tf_op jit(solution)/shard_map/all_to_all | solution.py:112
  209.0 4.5 %bitcast_reduce_fusion = bf16[192,2048]{1,0:T(8,128)(2,1)S(1)} fusion(bf16[192,1,2048]{2,1,0:T(2,128)(2,1)S(1)} %reshape.489), kind=kLoop, calls=%fused_computation.190 | loop fusion | bytes 1572864 | tf_op jit(solution)/shard_map/all_to_all | solution.py:112
  216.4 7.6 %fusion.14 = bf16[16,12,32,64]{3,0,2,1:T(8,128)(2,1)S(1)} fusion(f32[32]{0:T(128)S(1)} %copy-done.72, f32[12,16,32]{1,2,0:T(8,128)S(1)} %copy-done.43, f32[12,16,32]{1,2,0:T(8,128)S(1)} %copy-done.46, f32[12,16,16]{2,1,0:T(8,128)S(1)} %copy-done.50, pred[16,16]{1,0:T(8,128)(4,1)S(1)} %copy-done.70, bf16[16,12,32,64]{3,2,1,0:T(8,128)(2,1)S(1)} %reshape.451), kind=kOutput, calls=%fused_computation.34 | convolution fusion | flops 77463552 | bytes 1634688 | tf_op jit(solution)/shard_map/jvp(vmap(ijh,jhd->ihd))/dot_general | solution.py:52
  236.2 7.9 %fusion.31 = f32[3,1,32,64,64]{4,3,2,1,0:T(8,128)} fusion(bf16[3,64,64,1]{2,1,3,0:T(8,128)(2,1)S(1)} %bitcast.294, f32[3,64,32,64]{3,2,1,0:T(8,128)} %reshape.462, f32[3,64,32]{1,2,0:T(8,128)S(1)} %copy-done.28), kind=kOutput, calls=%fused_computation.62 | convolution fusion | flops 302383104 | bytes 3194880 | tf_op jit(solution)/shard_map/transpose(jvp(vmap(kin,khdn->kihd)))/dot_general | solution.py:38
  244.0 14.1 %all-to-all-done.3 = bf16[16,12,2048]{2,1,0:T(8,128)(2,1)} async-done(((bf16[16,12,2048]{2,1,0:T(8,128)(2,1)}), bf16[16,12,2048]{2,1,0:T(8,128)(2,1)}, u32[]{:S(2)}, u32[]{:S(2)}) %all-to-all-start.3) | async-done | bytes 786464 | tf_op jit(solution)/shard_map/all_to_all | solution.py:130
  264.8 11.0 %while.37 = (s32[]{:T(128)}, f32[1,32,64,64]{3,2,1,0:T(8,128)S(1)}, f32[3,1,32]{2,1,0:T(1,128)S(1)}, f32[3,1,32,64,64]{4,3,2,1,0:T(8,128)}, f32[3,1,32,64,64]{4,...) while((s32[]{:T(128)}, f32[1,32,64,64]{3,2,1,0:T(8,128)S(1)}, ...), condition=%wide.region_6.7_spmd.clone, body=%wide.region_4.6_spmd.clone.sunk | while | flops 786436 | bytes 3672220 | solution.py:34
  282.2 5.4 %fusion.5 = bf16[1,3,64,32,64]{2,4,3,1,0:T(8,128)(2,1)} fusion(f32[3,64,32,64]{1,3,2,0:T(8,128)S(1)} %fusion.33, f32[3,64,32]{1,2,0:T(8,128)S(1)} %copy-done.30, f32[3,64,32]{1,2,0:T(8,128)S(1)} %copy-done.55, f32[3,64,32]{1,2,0:T(8,128)S(1)} %copy-done.57, f32[3,64,64]{2,1,0:T(8,128)S(1)} %copy-done.53, pred[64,64]{1,0:T(8,128)(4,1)S(1)} %copy-done.64, ...), kind=kOutput, calls=%fused_computation.18 | convolution fusion | flops 304742400 | bytes 3272704 | tf_op jit(solution)/shard_map/transpose(jvp(vmap(kijh,kjhd->kihd)))/dot_general | solution.py:25
  294.5 5.5 %fusion.37 = (f32[3,64,32]{1,2,0:T(8,128)}, f32[3,64,32]{1,2,0:T(8,128)}, f32[3,64,32]{1,2,0:T(8,128)}, f32[3,64,64]{2,1,0:T(8,128)S(1)}) fusion(f32[3,64,64]{2,1,0:T(8,128)S(1)} %copy-done.53, f32[3,64,32]{1,2,0:T(8,128)} %copy.214, f32[3,64,32]{1,2,0:T(8,128)S(1)} %copy-done.55, pred[64,64]{1,0:T(8,128)(4,1)S(1)} %copy-done.64, ...), kind=kOutput, calls=%fused_computation.66 | convolution fusion | flops 55412736 | bytes 1798144 | tf_op jit(solution)/shard_map/transpose(jvp(vmap(kijh,kjhd->kihd)))/dot_general | solution.py:25
  300.7 5.3 %fusion.99 = bf16[1,3,64,64]{2,3,1,0:T(8,128)(2,1)S(1)} fusion(f32[1,3,64,64]{2,3,1,0:T(8,128)S(1)} %convolution_bitcast_fusion, bf16[3,64,32,64]{1,3,2,0:T(8,128)(2,1)S(1)} %copy-done.8, f32[3,64,32]{1,2,0:T(8,128)S(1)} %copy-done.30, f32[3,1,32,64,64]{4,3,2,1,0:T(8,128)S(1)} %copy-done.4), kind=kOutput, calls=%fused_computation.118 | convolution fusion | flops 302800896 | bytes 2457600 | tf_op jit(solution)/shard_map/transpose(jvp(vmap(kjh,kjhd,kjn->khdn)))/dot_general | solution.py:28
  319.2 7.7 %fusion.89 = f32[3,64,64]{2,1,0:T(8,128)S(1)} fusion(f32[3,1,32,64,64]{4,3,2,1,0:T(8,128)S(1)} %copy-done.3, f32[3,64,32,64]{3,2,1,0:T(8,128)} %reshape.462, f32[3,64,32]{1,2,0:T(8,128)S(1)} %copy-done.29), kind=kOutput, calls=%fused_computation.112 | convolution fusion | flops 302383104 | bytes 3219456 | tf_op jit(solution)/shard_map/transpose(jvp(vmap(kin,khdn->kihd)))/dot_general | solution.py:38
  337.7 6.1 %all-to-all-done.7 = bf16[16,2,192]{2,1,0:T(2,128)(2,1)S(1)} async-done(((bf16[16,2,192]{2,1,0:T(2,128)(2,1)}), bf16[16,2,192]{2,1,0:T(2,128)(2,1)S(1)}, u32[]{:S(2)}, u32[]{:S(2)}) %all-to-all-start.7) | async-done | bytes 12320 | tf_op jit(solution)/shard_map/all_to_all | solution.py:135
  348.4 7.0 %all-to-all-done.6 = bf16[16,12,128]{2,1,0:T(8,128)(2,1)S(1)} async-done(((bf16[16,12,128]{2,1,0:T(8,128)(2,1)}), bf16[16,12,128]{2,1,0:T(8,128)(2,1)S(1)}, u32[]{:S(2)}, u32[]{:S(2)}) %all-to-all-start.6) | async-done | bytes 49184 | tf_op jit(solution)/shard_map/all_to_all | solution.py:134
  (288 shorter events, 160.4 us)
Async XLA Ops:
  7.2 52.3 %copy-start = (bf16[1,192,1024]{2,1,0:T(8,128)(2,1)S(1)}, bf16[1,192,1024]{2,1,0:T(8,128)(2,1)}, u32[]{:S(2)}) copy-start(bf16[1,192,1024]{2,1,0:T(8,128)(2,1)} %param.17) | copy-start | bytes 1179652
  7.2 52.3 %all-gather.2.cloned.1.call-start = ((), (), s32[]{:S(2)}) async-start(), calls=%async_computation.9 | async-start | bytes 4456448 | tf_op jit(solution)/shard_map/all_gather | solution.py:103
  10.9 40.7 %all-to-all-start.2 = ((bf16[16,2,192]{2,1,0:T(2,128)(2,1)}), bf16[16,2,192]{2,1,0:T(2,128)(2,1)S(1)}, u32[]{:S(2)}, u32[]{:S(2)}) async-start(bf16[16,2,192]{2,1,0:T(2,128)(2,1)} %reshape.482), calls=%async_computation.2 | async-start | bytes 32768 | tf_op jit(solution)/shard_map/all_to_all | solution.py:116
  27.6 17.1 %copy-start.5 = (bf16[3,64,32,64]{3,2,1,0:T(8,128)(2,1)}, bf16[3,64,32,64]{3,2,1,0:T(8,128)(2,1)S(1)}, u32[]{:S(2)}) copy-start(bf16[3,64,32,64]{3,2,1,0:T(8,128)(2,1)S(1)} %reshape.449) | copy-start | bytes 2359300
  29.0 17.8 %copy-start.6 = (bf16[3,64,32,64]{1,3,2,0:T(8,128)(2,1)}, bf16[3,64,32,64]{1,3,2,0:T(8,128)(2,1)S(1)}, u32[]{:S(2)}) copy-start(bf16[3,64,32,64]{1,3,2,0:T(8,128)(2,1)S(1)} %copy.220) | copy-start | bytes 2359300
  51.6 22.2 %all-to-all-start.1 = ((bf16[16,2,768]{2,1,0:T(2,128)(2,1)}), bf16[16,2,768]{2,1,0:T(2,128)(2,1)S(1)}, u32[]{:S(2)}, u32[]{:S(2)}) async-start(bf16[16,2,768]{2,1,0:T(2,128)(2,1)} %reshape.484), calls=%async_computation.1 | async-start | bytes 98304 | tf_op jit(solution)/shard_map/all_to_all | solution.py:113
  64.5 16.9 %copy-start.21 = (bf16[1,192,64]{2,1,0:T(8,128)(2,1)S(1)}, bf16[1,192,64]{2,1,0:T(8,128)(2,1)}, u32[]{:S(2)}) copy-start(bf16[1,192,64]{2,1,0:T(8,128)(2,1)} %copy-done.20) | copy-start | bytes 73732
  64.5 16.9 %copy-start.23 = (bf16[1,192,64]{2,1,0:T(8,128)(2,1)S(1)}, bf16[1,192,64]{2,1,0:T(8,128)(2,1)}, u32[]{:S(2)}) copy-start(bf16[1,192,64]{2,1,0:T(8,128)(2,1)} %get-tuple-element.395) | copy-start | bytes 73732
  64.5 18.3 %copy-start.67 = (f32[32]{0:T(128)S(1)}, f32[32]{0:T(128)}, u32[]{:S(2)}) copy-start(f32[32]{0:T(128)} %get-tuple-element.401) | copy-start | bytes 388
  73.8 30.2 %all-to-all-start.4 = ((bf16[16,2,12288]{2,1,0:T(2,128)(2,1)}), bf16[16,2,12288]{2,1,0:T(2,128)(2,1)}, u32[]{:S(2)}, u32[]{:S(2)}) async-start(bf16[16,2,12288]{2,1,0:T(2,128)(2,1)} %reshape.486), calls=%async_computation.4 | async-start | bytes 1572864 | tf_op jit(solution)/shard_map/all_to_all | solution.py:117
  81.3 35.3 %copy-start.69 = (pred[16,16]{1,0:T(8,128)(4,1)}, pred[16,16]{1,0:T(8,128)(4,1)S(1)}, u32[]{:S(2)}) copy-start(pred[16,16]{1,0:T(8,128)(4,1)S(1)} %iota_compare_fusion.1) | copy-start | bytes 772
  82.8 33.8 %copy-start.42 = (f32[12,16,32]{1,2,0:T(8,128)}, f32[12,16,32]{1,2,0:T(8,128)S(1)}, u32[]{:S(2)}) copy-start(f32[12,16,32]{1,2,0:T(8,128)S(1)} %copy.232) | copy-start | bytes 73732
  83.0 33.6 %copy-start.45 = (f32[12,16,32]{1,2,0:T(8,128)}, f32[12,16,32]{1,2,0:T(8,128)S(1)}, u32[]{:S(2)}) copy-start(f32[12,16,32]{1,2,0:T(8,128)S(1)} %copy.230) | copy-start | bytes 73732
  84.3 32.3 %copy-start.49 = (f32[12,16,16]{2,1,0:T(8,128)}, f32[12,16,16]{2,1,0:T(8,128)S(1)}, u32[]{:S(2)}) copy-start(f32[12,16,16]{2,1,0:T(8,128)S(1)} %fusion.121) | copy-start | bytes 36868
  84.3 33.5 %copy-start.72 = (f32[32]{0:T(128)S(1)}, f32[32]{0:T(128)}, u32[]{:S(2)}) copy-start(f32[32]{0:T(128)} %param.15) | copy-start | bytes 388
  125.5 31.6 %all-to-all-start.5 = ((bf16[16,12,2048]{2,1,0:T(8,128)(2,1)}), bf16[16,12,2048]{2,1,0:T(8,128)(2,1)}, u32[]{:S(2)}, u32[]{:S(2)}) async-start(bf16[16,12,2048]{2,1,0:T(8,128)(2,1)} %reshape.471), calls=%async_computation.5 | async-start | bytes 2097152 | tf_op jit(solution)/shard_map/all_to_all | solution.py:131
  141.4 19.4 %copy-start.2 = (f32[3,1,32,64,64]{4,3,2,1,0:T(8,128)S(1)}, f32[3,1,32,64,64]{4,3,2,1,0:T(8,128)}, u32[]{:S(2)}) copy-start(f32[3,1,32,64,64]{4,3,2,1,0:T(8,128)} %get-tuple-element.537) | copy-start | bytes 4718596
  226.6 31.6 %all-to-all-start.3 = ((bf16[16,12,2048]{2,1,0:T(8,128)(2,1)}), bf16[16,12,2048]{2,1,0:T(8,128)(2,1)}, u32[]{:S(2)}, u32[]{:S(2)}) async-start(bf16[16,12,2048]{2,1,0:T(8,128)(2,1)} %reshape.470), calls=%async_computation.3 | async-start | bytes 2097152 | tf_op jit(solution)/shard_map/all_to_all | solution.py:130
  230.8 129.3 %reduce-scatter.2.cloned.1.call-start = ((), (), s32[]{:S(2)}) async-start(), calls=%async_computation.10 | async-start | bytes 4456448 | tf_op jit(solution)/shard_map/reduce_scatter | solution.py:143
  264.8 11.0 %copy-start.22 = (bf16[1,192,64]{2,1,0:T(8,128)(2,1)S(1)}, bf16[1,192,64]{2,1,0:T(8,128)(2,1)}, u32[]{:S(2)}) copy-start(bf16[1,192,64]{2,1,0:T(8,128)(2,1)} %copy-done.20) | copy-start | bytes 73732
  327.2 28.2 %copy-start.48 = (bf16[1,3,64,64]{3,2,1,0:T(8,128)(2,1)S(1)}, bf16[1,3,64,64]{3,2,1,0:T(8,128)(2,1)}, u32[]{:S(2)}) copy-start(bf16[1,3,64,64]{3,2,1,0:T(8,128)(2,1)} %copy.257) | copy-start | bytes 73732
  331.5 24.6 %copy-start.12 = (bf16[192,2048]{1,0:T(8,128)(2,1)S(1)}, bf16[192,2048]{1,0:T(8,128)(2,1)}, u32[]{:S(2)}) copy-start(bf16[192,2048]{1,0:T(8,128)(2,1)} %copy-done.11) | copy-start | bytes 2359300
  332.8 11.1 %all-to-all-start.7 = ((bf16[16,2,192]{2,1,0:T(2,128)(2,1)}), bf16[16,2,192]{2,1,0:T(2,128)(2,1)S(1)}, u32[]{:S(2)}, u32[]{:S(2)}) async-start(bf16[16,2,192]{2,1,0:T(2,128)(2,1)} %reshape.490), calls=%async_computation.7 | async-start | bytes 32768 | tf_op jit(solution)/shard_map/all_to_all | solution.py:135
  343.9 11.5 %all-to-all-start.6 = ((bf16[16,12,128]{2,1,0:T(8,128)(2,1)}), bf16[16,12,128]{2,1,0:T(8,128)(2,1)S(1)}, u32[]{:S(2)}, u32[]{:S(2)}) async-start(bf16[16,12,128]{2,1,0:T(8,128)(2,1)} %copy.260), calls=%async_computation.6 | async-start | bytes 131072 | tf_op jit(solution)/shard_map/all_to_all | solution.py:134
  (58 other events, 348.9 us)
Sparse Core Ops, SparseCore 0:
  9.8 46.3 all-gather.1
  262.9 57.0 reduce-scatter.1
where the time goes:
time: 376 us; the launch traced here: 369 us
  local copies, waits for them, and re-layouts  93.1 us (25%)
  matrix products  81.8 us (22%)
  waiting for transfers between devices  63.3 us (17%)
  other arithmetic  47.1 us (13%)
  starting transfers between devices  41.8 us (11%)
  blocking collectives  26.4 us (7%)
  between operations  15.4 us (4%)
    all_to_all x1, blocking collectives, on_device(): lax.all_to_all(spatial_bf, 'tm', split_axis=1, concat_axis=0, tiled=True)  26.4 us
    dot_general x3, matrix products, block_scan(): jnp.einsum('kin,khdn->kihd', c_blocks, entering, precision=HIGH)  23.9 us
    all_to_all x1, waiting for transfers between devices, on_device(): lax.all_to_all(carried, 'tm', split_axis=1, concat_axis=0, tiled=True)  19.6 us
    unnamed x161, local copies, waits for them, and re-layouts  19.3 us
    dot_general x3, matrix products, whole_scan(): return jnp.einsum('ijh,jhd->ihd', weights, heads_in, precision=HIGH)  17 us
    all_to_all x1, waiting for transfers between devices, on_device(): lax.all_to_all(grad_spatial32.astype(jnp.bfloat16), 'tm', split_axis=0, c...  15.7 us
    dot_general x3, matrix products, block_scan(): inside = jnp.einsum('kijh,kjhd->kihd', weights, x_blocks, precision=HIGH)  15 us
    all_to_all x1, waiting for transfers between devices, on_device(): lax.all_to_all(mixed_bf, 'tm', split_axis=0, concat_axis=1, tiled=True)  14.1 us
  transfers between devices with their start and end apart: 9, of which 5 were waited for; matrix products, arithmetic and copies ran while one was open for 40% of the time, Pallas kernels for 0%

commit v1 on v0

v1 whole, which is shorter than its diff:
```python
import jax
import jax.numpy as jnp
from jax import lax
from jax.experimental import pallas as pl
from jax.experimental.pallas import tpu as pltpu
from jax.sharding import PartitionSpec as P

F32 = jnp.float32
BF16 = jnp.bfloat16
LOG2E = 1.4426950408889634
CAP = 8.0

ROWS = 192
HEADS = 32
PAIRS = 16
MODEL = 1024
FRAMES = 16
PATCHES = 12
TILES = MODEL // 128
SENT = PAIRS + TILES + 2
HIGH = lax.Precision.HIGHEST
MIB = 1024 * 1024

SPATIAL_FWD = (((0, 128), (0, 128)), ((128, 192), (0, 192)))
SPATIAL_BWD = (((0, 128), (0, 192)), ((128, 192), (128, 192)))
TEMPORAL = (((0, 128), (0, 128)), ((128, 192), (128, 192)))


def dot(a, b, contract=((1,), (0,)), precision=None):
    return lax.dot_general(
        a, b, (contract, ((), ())), precision=precision, preferred_element_type=F32
    )


def mask_of(temporal, transposed=False):
    i = lax.broadcasted_iota(jnp.int32, (ROWS, ROWS), 1 if transposed else 0)
    j = lax.broadcasted_iota(jnp.int32, (ROWS, ROWS), 0 if transposed else 1)
    keep = i >= j
    if temporal:
        keep = keep & ((i >> 4) == (j >> 4))
    return keep


def softplus(v):
    return jnp.maximum(v, 0.0) + jnp.log1p(jnp.exp(-jnp.abs(v)))


def decay_terms(raw, rate, temporal):
    step = softplus(raw)
    cum = dot(mask_of(temporal).astype(F32), step * rate, precision=HIGH) * (-LOG2E)
    return step, cum, jnp.log(step) * LOG2E - cum


def head_lanes(shape):
    return lax.broadcasted_iota(jnp.int32, shape, 1) < 64


def split_pair(v):
    low = head_lanes(v.shape)
    zero = jnp.zeros_like(v)
    return jnp.where(low, v, zero), jnp.where(low, zero, v)


def both_heads(pair, one_head):
    return jnp.concatenate([one_head(2 * pair), one_head(2 * pair + 1)], axis=0)


def pick_heads(v):
    return jnp.where(head_lanes((ROWS, 128)), v[:ROWS], v[ROWS:])


def padded(parts, block, lanes):
    out = []
    for v, (_, (c0, c1)) in zip(parts, block):
        row = [jnp.zeros((v.shape[0], c0), v.dtype)] if c0 else []
        row.append(v)
        if c1 < lanes:
            row.append(jnp.zeros((v.shape[0], lanes - c1), v.dtype))
        out.append(jnp.concatenate(row, axis=1) if len(row) > 1 else v)
    return jnp.concatenate(out, axis=0)


def scan_forward(blocks, gram, cum, from_row, x_pair, pair):
    def weights(h):
        parts = []
        for (i0, i1), (j0, j1) in blocks:
            e = jnp.exp2(jnp.minimum(cum[i0:i1, h : h + 1] + from_row[h : h + 1, j0:j1], CAP))
            parts.append((e * gram[i0:i1, j0:j1]).astype(BF16))
        return padded(parts, blocks, ROWS)

    return pick_heads(dot(both_heads(pair, weights), x_pair))


def scan_backward(blocks, gram_t, cum_row, from_col, x_pair, dy_pair, pair, dgram, rowsum, colsum):
    products = dot(jnp.concatenate(split_pair(x_pair), axis=0), dy_pair, ((1,), (1,)))
    added = [None] * len(blocks)

    def weights(h):
        parts = []
        sums = []
        for n, ((j0, j1), (i0, i1)) in enumerate(blocks):
            e = jnp.exp2(jnp.minimum(from_col[j0:j1, h : h + 1] + cum_row[h : h + 1, i0:i1], CAP))
            w = e * gram_t[j0:j1, i0:i1]
            base = ROWS * (h - 2 * pair)
            p = products[base + j0 : base + j1, i0:i1]
            t = p * e
            added[n] = t if added[n] is None else added[n] + t
            m = p * w
            colsum[j0:j1, h : h + 1] = jnp.sum(m, axis=1, keepdims=True)
            sums.append((i0, i1, jnp.sum(m, axis=0, keepdims=True)))
            parts.append(w.astype(BF16))
        (a0, a1, first), (b0, b1, second) = sums
        if b0 < a1:
            rowsum[h : h + 1, a0:b0] = first[:, : b0 - a0]
            rowsum[h : h + 1, b0:b1] = first[:, b0 - a0 :] + second
        else:
            rowsum[h : h + 1, a0:a1] = first
            rowsum[h : h + 1, b0:b1] = second
        return padded(parts, blocks, ROWS)

    dx = pick_heads(dot(both_heads(pair, weights), dy_pair))
    for ((j0, j1), (i0, i1)), t in zip(blocks, added):
        dgram[j0:j1, i0:i1] += t
    return dx


def finish_backward(temporal, dgram, rowsum, colsum, b, c, raw, step, rate):
    dg = jnp.where(mask_of(temporal, True), dgram[...], 0.0).astype(BF16)
    db = dot(dg, c)
    dc = dot(dg, b, ((0,), (0,)))
    col = colsum[...]
    dcum = rowsum[...].T - col
    dlog = dot(mask_of(temporal, True).astype(F32), dcum, precision=HIGH)
    dstep = col / step - rate * dlog
    draw = dstep / (1.0 + jnp.exp(-raw))
    return jnp.concatenate([db, dc], axis=1), draw


def put_spatial(wide, row, v):
    wide[pl.ds(row, ROWS, stride=SENT), :] = v


def get_spatial(wide, row):
    return wide[pl.ds(row, ROWS, stride=SENT), :]


def put_temporal(wide, row, v):
    for p in range(PATCHES):
        wide[pl.ds(p * SENT + row, FRAMES, stride=PATCHES * SENT), :] = v[16 * p : 16 * p + 16]


def get_temporal(wide, row):
    return jnp.concatenate(
        [wide[pl.ds(p * SENT + row, FRAMES, stride=PATCHES * SENT), :] for p in range(PATCHES)], axis=0
    )


def spatial_forward_kernel(
    x_hbm, bc_hbm, raw_hbm, grad_hbm, rate_ref, out_ref, wide, x_ref, bc_ref, raw_ref, grad_ref, sems
):
    def load(n, src, dst):
        copy = pltpu.make_async_copy(src, dst, sems.at[n])
        copy.start()
        return copy

    maps = load(0, bc_hbm, bc_ref)
    steps = load(1, raw_hbm, raw_ref)
    quarters = [pl.ds(512 * q, 512) for q in range(4)]
    xs = [load(2 + q, x_hbm.at[:, quarters[q]], x_ref.at[:, quarters[q]]) for q in range(4)]
    grads = load(6, grad_hbm, grad_ref)
    steps.wait()
    raw = raw_ref[...].astype(F32).T
    put_spatial(wide, PAIRS + TILES + 1, jnp.concatenate([raw, jnp.zeros_like(raw)], axis=1))
    _, cum, from_col = decay_terms(raw[:, :HEADS], rate_ref[0:1, :], False)
    from_row = from_col.T
    maps.wait()
    put_spatial(wide, PAIRS + TILES, bc_ref[:, 128:].astype(F32))
    gram = dot(bc_ref[:, 64:128], bc_ref[:, 0:64], ((1,), (1,)))
    gram = jnp.where(mask_of(False), gram, 0.0)
    for g in range(PAIRS):
        if g % 4 == 0:
            xs[g // 4].wait()
        y = scan_forward(SPATIAL_FWD, gram, cum, from_row, x_ref[:, 128 * g : 128 * g + 128], g)
        put_spatial(wide, g, y)
    grads.wait()
    for k in range(TILES):
        put_spatial(wide, PAIRS + k, grad_ref[:, 128 * k : 128 * k + 128].astype(F32))
    out_ref[...] = wide[...].astype(BF16)


def weight_grad(mixed_ref, grad_ref, parity, column):
    lanes = [pl.ds(pl.multiple_of((2 * z + parity) * 128, 128), 128) for z in range(PAIRS // 2)]
    rows = jnp.concatenate([mixed_ref[:, at] for at in lanes], axis=1)
    return dot(rows, grad_ref[:, column : column + 256], ((0,), (0,)))


def temporal_forward_kernel(
    core_ref, here_ref, rate_ref, gain_ref,
    x_out, mixed_out, grad_out, bc_out, raw_out, other_out,
    wide, x_ref, mixed_ref, grad_ref, bc_ref, raw_ref, other_ref, sems,
):
    saves = []

    def save(src, dst):
        copy = pltpu.make_async_copy(src, dst, sems.at[len(saves)])
        copy.start()
        saves.append(copy)

    wide[...] = here_ref[...].astype(F32)
    for k in range(TILES):
        grad_ref[:, 128 * k : 128 * k + 128] = get_temporal(wide, PAIRS + k).astype(BF16)
    save(grad_ref, grad_out)
    bc = get_temporal(wide, PAIRS + TILES).astype(BF16)
    bc_ref[...] = bc
    save(bc_ref, bc_out)
    raw = get_temporal(wide, PAIRS + TILES + 1)
    raw_ref[...] = raw
    save(raw_ref, raw_out)
    _, cum, from_col = decay_terms(raw[:, HEADS : 2 * HEADS], rate_ref[1:2, :], True)
    from_row = from_col.T
    gram = dot(bc[:, 64:128], bc[:, 0:64], ((1,), (1,)))
    gram = jnp.where(mask_of(True), gram, 0.0)
    low = head_lanes((1, 128))
    for g in range(PAIRS):
        x = get_temporal(wide, g)
        xb = x.astype(BF16)
        x_ref[:, 128 * g : 128 * g + 128] = xb
        y = scan_forward(TEMPORAL, gram, cum, from_row, xb, g)
        gain = jnp.where(low, gain_ref[0, 2 * g], gain_ref[0, 2 * g + 1])
        mixed_ref[:, 128 * g : 128 * g + 128] = (y + gain * x).astype(BF16)
    save(x_ref, x_out)
    save(mixed_ref, mixed_out)
    for column in range(0, MODEL, 256):
        dw = weight_grad(mixed_ref, grad_ref, 1 - core_ref[0], column)
        other_ref[:, :, column : column + 256] = dw.reshape(8, 128, 256).astype(BF16)
    save(other_ref, other_out)
    for copy in saves:
        copy.wait()


def weight_grad_kernel(
    core_ref, mixed_hbm, grad_hbm, got_ref, back_in, out_ref, back_out, mixed_ref, grad_ref, sems
):
    del back_in, back_out
    loads = [
        pltpu.make_async_copy(mixed_hbm, mixed_ref, sems.at[0]),
        pltpu.make_async_copy(grad_hbm, grad_ref, sems.at[1]),
    ]
    for copy in loads:
        copy.start()
    for copy in loads:
        copy.wait()
    for column in range(0, MODEL, 256):
        at = slice(column, column + 256)
        dw = weight_grad(mixed_ref, grad_ref, core_ref[0], column).reshape(8, 128, 256)
        out_ref[:, :, at] = (dw + got_ref[:, :, at].astype(F32)).astype(BF16)


def temporal_backward_kernel(
    place_ref, x_hbm, mixed_hbm, grad_hbm, bc_hbm, raw_hbm, mine_hbm, theirs_hbm, rate_ref, gain_ref,
    out_ref, wide, weight, dy_all, x_ref, mixed_ref, grad_ref, bc_ref, raw_ref,
    dgram, rowsum, colsum, sems,
):
    core, x, y = place_ref[0], place_ref[1], place_ref[2]
    pairs = [
        (raw_hbm, raw_ref),
        (bc_hbm, bc_ref),
        (grad_hbm, grad_ref),
        (x_hbm, x_ref),
        (mixed_hbm, mixed_ref),
    ]
    for src, half in ((mine_hbm, core), (theirs_hbm, 1 - core)):
        for a in range(4):
            for b in range(4):
                from_x = x ^ (a + half * (b - a))
                from_y = y ^ (b + half * (a - b))
                at = pl.ds(pl.multiple_of(256 * from_y, 256), 256)
                pairs.append((src.at[a, b], weight.at[:, half, from_x, :, at]))
    loads = [pltpu.make_async_copy(src, dst, sems.at[n]) for n, (src, dst) in enumerate(pairs)]
    for copy in loads:
        copy.start()
    loads[0].wait()
    raw = raw_ref[:, HEADS : 2 * HEADS]
    rate = rate_ref[1:2, :]
    step, cum, from_col = decay_terms(raw, rate, True)
    cum_row = cum.T
    loads[1].wait()
    b, c = bc_ref[:, 0:64], bc_ref[:, 64:128]
    gram_t = jnp.where(mask_of(True, True), dot(b, c, ((1,), (1,))), 0.0)
    dgram[...] = jnp.zeros_like(dgram)
    low = head_lanes((1, 128))
    for copy in loads[2:]:
        copy.wait()
    for z in range(PAIRS // 2):
        w = weight[2 * z : 2 * z + 2].reshape(256, MODEL)
        dy_all[:, 256 * z : 256 * z + 256] = dot(grad_ref[...], w, ((1,), (1,))).astype(BF16)
    for g in range(PAIRS):
        dy = dy_all[:, 128 * g : 128 * g + 128]
        dx = scan_backward(
            TEMPORAL, gram_t, cum_row, from_col, x_ref[:, 128 * g : 128 * g + 128], dy, g,
            dgram, rowsum, colsum,
        )
        gain = jnp.where(low, gain_ref[0, 2 * g], gain_ref[0, 2 * g + 1])
        put_temporal(wide, g, dx + gain * dy.astype(F32))
    dbc, draw = finish_backward(True, dgram, rowsum, colsum, b, c, raw, step, rate)
    put_temporal(wide, PAIRS + TILES, dbc)
    put_temporal(
        wide, PAIRS + TILES + 1, jnp.concatenate([draw, jnp.zeros((ROWS, 128 - HEADS), F32)], axis=1)
    )
    for k in range(0, TILES, 2):
        w = weight[:, :, :, :, 128 * k : 128 * k + 256].reshape(2048, 256)
        projected = dot(mixed_ref[...], w)
        for t in range(2):
            put_temporal(wide, PAIRS + k + t, projected[:, 128 * t : 128 * t + 128])
    out_ref[...] = wide[...].astype(BF16)


def spatial_backward_kernel(
    x_ref, back_ref, bc_ref, raw_ref, rate_ref, out_ref, dx_ref, dbc_ref, draw_ref,
    wide, dgram, rowsum, colsum,
):
    wide[...] = back_ref[...].astype(F32)
    for k in range(TILES):
        out_ref[:, 128 * k : 128 * k + 128] = get_spatial(wide, PAIRS + k).astype(BF16)
    raw = raw_ref[...].astype(F32).T[:, :HEADS]
    rate = rate_ref[0:1, :]
    step, cum, from_col = decay_terms(raw, rate, False)
    cum_row = cum.T
    b, c = bc_ref[:, 0:64], bc_ref[:, 64:128]
    gram_t = jnp.where(mask_of(False, True), dot(b, c, ((1,), (1,))), 0.0)
    dgram[...] = jnp.zeros_like(dgram)
    for g in range(PAIRS):
        dy = get_spatial(wide, g).astype(BF16)
        dx = scan_backward(
            SPATIAL_BWD, gram_t, cum_row, from_col, x_ref[:, 128 * g : 128 * g + 128], dy, g,
            dgram, rowsum, colsum,
        )
        dx_ref[:, 128 * g : 128 * g + 128] = dx.astype(BF16)
    dbc, draw = finish_backward(False, dgram, rowsum, colsum, b, c, raw, step, rate)
    dbc_ref[:, 0:128] = dbc.astype(BF16)
    dbc_ref[:, 128:256] = get_spatial(wide, PAIRS + TILES).astype(BF16)
    draw_t = get_spatial(wide, PAIRS + TILES + 1)
    draw_ref[...] = jnp.concatenate([draw, draw_t[:, :HEADS]], axis=1).T.astype(BF16)


def shape(*dims, dtype=BF16):
    return jax.ShapeDtypeStruct(dims, dtype)


def scan_scratch():
    return [
        pltpu.VMEM((ROWS, ROWS), F32),
        pltpu.VMEM((HEADS, ROWS), F32),
        pltpu.VMEM((ROWS, HEADS), F32),
    ]


def smem():
    return pl.BlockSpec(memory_space=pltpu.SMEM)


def vmem(n):
    return [pl.BlockSpec(memory_space=pltpu.VMEM)] * n


def exchange(v):
    blocks = v.reshape(16, v.shape[0] // 16, 128)
    return lax.all_to_all(blocks, "tm", 0, 0, tiled=True).reshape(v.shape)


def hbm(n):
    return [pl.BlockSpec(memory_space=pltpu.HBM)] * n


def call(kernel, outs, in_specs, scratch, us, mib, out_specs=None, aliases={}):
    more = {} if out_specs is None else {"out_specs": tuple(out_specs)}
    return pl.pallas_call(
        kernel,
        **more,
        input_output_aliases=aliases,
        out_shape=outs,
        in_specs=in_specs,
        scratch_shapes=scratch,
        compiler_params=pltpu.CompilerParams(vmem_limit_bytes=mib * MIB),
        cost_estimate=pl.CostEstimate(
            flops=int(us * 1.0e9), bytes_accessed=int(us * 3.0e6), transcendentals=0
        ),
    )


def across(axis, v, bit):
    return lax.ppermute(v, axis, [(s, s ^ bit) for s in range(16)])


def in_hbm(*arrays):
    return [pltpu.with_memory_space_constraint(v, pltpu.HBM) for v in arrays]


def pass_kernel(v_in, token, v_out):
    del v_in, token, v_out


def after(v, token):
    return pl.pallas_call(
        pass_kernel,
        out_shape=pltpu.HBM(v.shape, v.dtype),
        in_specs=hbm(2),
        out_specs=hbm(1)[0],
        input_output_aliases={0: 0},
    )(*in_hbm(v, token))


def weight_part(w_out):
    clip = lax.axis_index("clip")
    mine = lax.dynamic_slice(
        w_out.reshape(2, 64, MODEL), (0, 16 * (clip // 4), 256 * lax.rem(clip, 4)), (2, 16, 256)
    )
    return lax.all_to_all(jnp.tile(mine, (8, 1, 1)), "tm", 0, 0, tiled=True)


def gather_weight(part):
    for step in range(2):
        got = [part]
        for bits in (1, 2, 3):
            to = []
            for device in range(256):
                along_x = (device % 2) != step
                to.append((device, device ^ ((bits * 64) if along_x else (bits * 16))))
            got.append(lax.ppermute(part, ("clip", "tm"), to))
        part = jnp.stack(got)
    return part, across("tm", part, 1)


def on_device(x_inner, bc_inputs, step_raw, decay_rate, skip_gain, w_out, grad_out):
    x, bc, grad = x_inner[0], bc_inputs[0], grad_out[0]
    raw = step_raw[0].T
    gain = skip_gain.reshape(1, HEADS)
    tm, clip = lax.axis_index("tm"), lax.axis_index("clip")
    core = jnp.stack([lax.rem(tm, 2), clip // 4, lax.rem(clip, 4)]).astype(jnp.int32)
    along_z = [[2 * z + c for z in range(8)] for c in range(2)]
    wide = pltpu.VMEM((ROWS * SENT, 128), F32)

    part = weight_part(w_out)
    ahead = call(
        spatial_forward_kernel,
        shape(ROWS * SENT, 128),
        hbm(4) + vmem(1),
        [
            wide,
            pltpu.VMEM((ROWS, 2048), BF16),
            pltpu.VMEM((ROWS, 256), BF16),
            pltpu.VMEM((2 * HEADS, ROWS), BF16),
            pltpu.VMEM((ROWS, MODEL), BF16),
            pltpu.SemaphoreType.DMA((7,)),
        ],
        4,
        16,
    )(*in_hbm(x, bc, raw, grad), decay_rate)
    mine, theirs = gather_weight(after(part, ahead))
    ahead = exchange(ahead)

    kept = [(ROWS, 2048), (ROWS, 2048), (ROWS, MODEL), (ROWS, 128), (ROWS, 128), (8, 128, MODEL)]
    types = [BF16, BF16, BF16, BF16, F32, BF16]
    x_t, mixed, grad_t, bc_t, raw_t, other = call(
        temporal_forward_kernel,
        tuple(pltpu.HBM(dims, dtype) for dims, dtype in zip(kept, types)),
        [smem()] + vmem(2) + [smem()],
        [wide]
        + [pltpu.VMEM(dims, dtype) for dims, dtype in zip(kept, types)]
        + [pltpu.SemaphoreType.DMA((6,))],
        4,
        20,
        out_specs=hbm(6),
    )(core, ahead, decay_rate, gain)

    got = across("tm", other, 1)
    back = call(
        temporal_backward_kernel,
        shape(ROWS * SENT, 128),
        [smem()] + hbm(7) + vmem(1) + [smem()],
        [wide, pltpu.VMEM((16, 2, 4, 16, MODEL), BF16), pltpu.VMEM((ROWS, 2048), BF16)]
        + [pltpu.VMEM(dims, dtype) for dims, dtype in zip(kept[:5], types)]
        + scan_scratch()
        + [pltpu.SemaphoreType.DMA((37,))],
        7,
        24,
    )(core, *in_hbm(x_t, mixed, grad_t, bc_t, raw_t, mine, theirs), decay_rate, gain)

    partial, back = call(
        weight_grad_kernel,
        (shape(8, 128, MODEL), pltpu.HBM((ROWS * SENT, 128), BF16)),
        [smem()] + hbm(2) + vmem(1) + hbm(1),
        [pltpu.VMEM((ROWS, 2048), BF16), pltpu.VMEM((ROWS, MODEL), BF16), pltpu.SemaphoreType.DMA((2,))],
        2,
        14,
        out_specs=vmem(1) + hbm(1),
        aliases={4: 1},
    )(core, *in_hbm(mixed, grad_t), got, *in_hbm(back))
    grad_w = lax.psum_scatter(
        partial, "tm", scatter_dimension=0, axis_index_groups=along_z, tiled=False
    )
    back = exchange(back)

    mixed_out, grad_x, grad_bc, grad_step = call(
        spatial_backward_kernel,
        (shape(ROWS, MODEL), shape(ROWS, 2048), shape(ROWS, 256), shape(2 * HEADS, ROWS)),
        vmem(5),
        [wide] + scan_scratch(),
        8,
        18,
    )(x, back, bc, raw, decay_rate)
    return (mixed_out[None], grad_x[None], grad_bc[None], grad_step.T[None], grad_w.astype(F32))


def solution(mesh):
    rows = P(("clip", "tm"), None, None)
    return jax.shard_map(
        on_device,
        mesh=mesh,
        in_specs=(rows, rows, rows, P(), P(), P("tm", None), rows),
        out_specs=(rows, rows, rows, rows, P(("clip", "tm"), None)),
        check_vma=False,
    )
```

time: 376 us -> 152 us (0.40); the launches traced: 369 us -> 152 us
  local copies, waits for them, and re-layouts: 93.1 us -> 4.58 us
  matrix products: 81.8 us -> 0 us
  other arithmetic: 47.1 us -> 4.42 us
  waiting for transfers between devices: 63.3 us -> 24.1 us
  Pallas kernels: 0 us -> 31.2 us
  blocking collectives: 26.4 us -> 49.9 us
  starting transfers between devices: 41.8 us -> 23.3 us
    dot_general x21 -> x0, matrix products: 81.8 us -> none  [the longest x3 23.9 us: block_scan(): jnp.einsum('kin,khdn->kihd', c_blocks, entering, precision=HIGH)]
    all_to_all x7 -> x2, waiting for transfers between devices: 62.5 us -> 6.5 us  [the longest x1 3.56 us: weight_part(): return lax.all_to_all(jnp.tile(mine, (8, 1, 1)), 'tm', 0, 0, tiled=True)]
    pallas_call x0 -> x6, Pallas kernels: none -> 31.2 us  [the longest x1 8.67 us: on_device(): call(spatial_backward_kernel, (shape(ROWS, MODEL), shape(ROWS, 2048), sha...]
    all_to_all x7 -> x2, starting transfers between devices: 41.7 us -> 13.7 us  [the longest x1 9.98 us: weight_part(): return lax.all_to_all(jnp.tile(mine, (8, 1, 1)), 'tm', 0, 0, tiled=True)]
    all_to_all x1, blocking collectives: 26.4 us -> 49.9 us  [exchange(): return lax.all_to_all(blocks, 'tm', 0, 0, tiled=True).reshape(v.shape)]
    convert_element_type x11 -> x0, local copies, waits for them, and re-layouts: 19 us -> none  [the longest x2 6.91 us: on_device(): grad_x32.astype(jnp.bfloat16)]
    ppermute x0 -> x8, waiting for transfers between devices: none -> 17.6 us  [the longest x6 17.6 us: gather_weight(): got.append(lax.ppermute(part, ('clip', 'tm'), to))]
    unnamed x161 -> x20, local copies, waits for them, and re-layouts: 19.3 us -> 3.91 us
  transfers between devices with their start and end apart: 9 -> 11, of which waited for: 5 -> 6; matrix products, arithmetic and copies ran while one was open for 40% -> 2% of each run, Pallas kernels for 0% -> 18%
where the time goes in v1:
time: 152 us
  blocking collectives  49.9 us (33%)
  Pallas kernels  31.2 us (21%)
  waiting for transfers between devices  24.1 us (16%)
  starting transfers between devices  23.3 us (15%)
  between operations  14.2 us (9%)
  local copies, waits for them, and re-layouts  4.58 us (3%)
  other arithmetic  4.42 us (3%)
    all_to_all x1, blocking collectives, exchange(): return lax.all_to_all(blocks, 'tm', 0, 0, tiled=True).reshape(v.shape)  49.9 us
    ppermute x6, waiting for transfers between devices, gather_weight(): got.append(lax.ppermute(part, ('clip', 'tm'), to))  17.6 us
    all_to_all x1, starting transfers between devices, weight_part(): return lax.all_to_all(jnp.tile(mine, (8, 1, 1)), 'tm', 0, 0, tiled=True)  9.98 us
    pallas_call x1, Pallas kernels, on_device(): call(spatial_backward_kernel, (shape(ROWS, MODEL), shape(ROWS, 2048), sha...  8.67 us
    pallas_call x1, Pallas kernels, on_device(): call(temporal_backward_kernel, shape(ROWS * SENT, 128), [smem()] + hbm(7)...  8.4 us
    ppermute x6, starting transfers between devices, gather_weight(): got.append(lax.ppermute(part, ('clip', 'tm'), to))  6.68 us
    pallas_call x1, Pallas kernels, on_device(): call(temporal_forward_kernel, tuple((pltpu.HBM(dims, dtype) for dims, dty...  5.26 us
    pallas_call x1, Pallas kernels, on_device(): call(spatial_forward_kernel, shape(ROWS * SENT, 128), hbm(4) + vmem(1), [...  4.92 us
  transfers between devices with their start and end apart: 11, of which 6 were waited for; matrix products, arithmetic and copies ran while one was open for 2% of the time, Pallas kernels for 18%

profile of v1, /device:TPU:1, one launch (start us, length us, event | category | flops | bytes accessed | tf_op | source)
XLA Modules:
  0.0 151.7 jit_solution(9170627469362253782)
XLA Ops:
  7.2 0.9 copy-done
  8.1 0.7 tile.4
  8.8 10.0 %all-to-all-start.1 = ((bf16[16,16,256]{2,1,0:T(8,128)(2,1)}), bf16[16,16,256]{2,1,0:T(8,128)(2,1)S(1)}, u32[]{:S(2)}, u32[]{:S(2)}) async-start(bf16[16,16,256]{2,1,0:T(8,128)(2,1)} %bitcast.12), calls=%async_computation.1 | async-start | bytes 262144 | tf_op jit(solution)/shard_map/all_to_all | solution.py:418
  18.8 0.7 copy-done.6
  19.5 4.9 %shard_map.110.token = bf16[4992,128]{1,0:T(8,128)(2,1)} custom-call(bf16[192,2048]{1,0:T(8,128)(2,1)} %bitcast.38, bf16[192,256]{1,0:T(8,128)(2,1)} %bitcast.40, bf16[64,192]{1,0:T(8,128)(2,1)} %bitcast.42, bf16[192,1024]{1,0:T(8,128)(2,1)} %bitcast.53, f32[2,32]{1,0:T(2,128)S(1)} %copy-done.6), custom_call_target="tpu_custom_call" | custom-call | flops 4000000000 | bytes 12000000 | tf_op jit(solution)/shard_map/pallas_call | solution.py:444
  24.4 3.6 %all-to-all-done.1.v_in = bf16[16,16,256]{2,1,0:T(8,128)(2,1)S(1)} async-done(((bf16[16,16,256]{2,1,0:T(8,128)(2,1)}), bf16[16,16,256]{2,1,0:T(8,128)(2,1)S(1)}, u32[]{:S(2)}, u32[]{:S(2)}) %all-to-all-start.1) | async-done | bytes 131104 | tf_op jit(solution)/shard_map/all_to_all | solution.py:418
  27.9 3.7 %all-to-all-start = ((bf16[16,312,128]{2,1,0:T(8,128)(2,1)}), bf16[16,312,128]{2,1,0:T(8,128)(2,1)S(1)}, u32[]{:S(2)}, u32[]{:S(2)}) async-start(bf16[16,312,128]{2,1,0:T(8,128)(2,1)} %bitcast.8), calls=%async_computation | async-start | bytes 2555904 | tf_op jit(solution)/shard_map/all_to_all | solution.py:368
  31.7 2.6 %collective-permute-start.3 = (bf16[16,16,256]{2,1,0:T(8,128)(2,1)}, bf16[16,16,256]{2,1,0:T(8,128)(2,1)S(1)}, u32[]{:S(2)}, u32[]{:S(2)}) collective-permute-start(bf16[16,16,256]{2,1,0:T(8,128)(2,1)} %shard_map.112), channel_id=1, source_target_pairs={{0,48},{1,193},{2,50},{3,195},{4,52},{5,197},{6,54},{7,199},{8,56}... | collective-permute-start | bytes 393224 | tf_op jit(solution)/shard_map/ppermute | solution.py:429
  35.0 2.9 %collective-permute-done.3 = bf16[16,16,256]{2,1,0:T(8,128)(2,1)S(1)} collective-permute-done((bf16[16,16,256]{2,1,0:T(8,128)(2,1)}, bf16[16,16,256]{2,1,0:T(8,128)(2,1)S(1)}, u32[]{:S(2)}, u32[]{:S(2)}) %collective-permute-start.3) | collective-permute-done | bytes 131104 | tf_op jit(solution)/shard_map/ppermute | solution.py:429
  37.9 2.2 %collective-permute-done.2 = bf16[16,16,256]{2,1,0:T(8,128)(2,1)S(1)} collective-permute-done((bf16[16,16,256]{2,1,0:T(8,128)(2,1)}, bf16[16,16,256]{2,1,0:T(8,128)(2,1)S(1)}, u32[]{:S(2)}, u32[]{:S(2)}) %collective-permute-start.2) | collective-permute-done | bytes 131104 | tf_op jit(solution)/shard_map/ppermute | solution.py:429
  40.1 1.0 fusion
  41.1 2.5 %collective-permute-start.6 = (bf16[4,16,16,256]{3,2,1,0:T(8,128)(2,1)S(1)}, bf16[4,16,16,256]{3,2,1,0:T(8,128)(2,1)S(1)}, u32[]{:S(2)}, u32[]{:S(2)}) collective-permute-start(bf16[4,16,16,256]{3,2,1,0:T(8,128)(2,1)S(1)} %get-tuple-element.30), channel_id=1, source_target_pairs={{0,192},{1,49},{2,194},{3,51},{4,196},{5,53},{6,198},{7,55},{8,200... | collective-permute-start | bytes 1572872 | tf_op jit(solution)/shard_map/ppermute | solution.py:429
  44.4 11.9 %collective-permute-done.6 = bf16[4,16,16,256]{3,2,1,0:T(8,128)(2,1)S(1)} collective-permute-done((bf16[4,16,16,256]{3,2,1,0:T(8,128)(2,1)S(1)}, bf16[4,16,16,256]{3,2,1,0:T(8,128)(2,1)S(1)}, u32[]{:S(2)}, u32[]{:S(2)}) %collective-permute-start.6) | collective-permute-done | bytes 524320 | tf_op jit(solution)/shard_map/ppermute | solution.py:429
  57.0 1.6 %pad_maximum_fusion.mine_hbm = bf16[4,4,16,16,256]{4,3,2,1,0:T(8,128)(2,1)} fusion(bf16[1,4,16,16,256]{4,3,2,1,0:T(8,128)(2,1)S(1)} %bitcast.47, bf16[1,4,16,16,256]{4,3,2,1,0:T(8,128)(2,1)S(1)} %bitcast.48, bf16[1,4,16,16,256]{4,3,2,1,0:T(8,128)(2,1)S(1)} %bitcast.49, bf16[1,4,16,16,256]{4,3,2,1,0:T(8,128)(2,1)S(1)} %get-tuple-element.29), kind=kLoop, calls=%fused_computation | loop fusion | flops 3145728 | bytes 4194304 | tf_op jit(solution)/shard_map/stack | solution.py:430
  58.5 2.6 %collective-permute-start.7 = (bf16[4,4,16,16,256]{4,3,2,1,0:T(8,128)(2,1)}, bf16[4,4,16,16,256]{4,3,2,1,0:T(8,128)(2,1)}, u32[]{:S(2)}, u32[]{:S(2)}) collective-permute-start(bf16[4,4,16,16,256]{4,3,2,1,0:T(8,128)(2,1)} %pad_maximum_fusion.mine_hbm), channel_id=1, source_target_pairs={{0,1},{1,0},{2,3},{3,2},{4,5},{5,4},{6,7},{7,6},{8,9},{9,8},{10,11... | collective-permute-start | bytes 6291464 | tf_op jit(solution)/shard_map/ppermute | solution.py:392
  61.2 2.9 %all-to-all-done = bf16[16,312,128]{2,1,0:T(8,128)(2,1)S(1)} async-done(((bf16[16,312,128]{2,1,0:T(8,128)(2,1)}), bf16[16,312,128]{2,1,0:T(8,128)(2,1)S(1)}, u32[]{:S(2)}, u32[]{:S(2)}) %all-to-all-start) | async-done | bytes 1277984 | tf_op jit(solution)/shard_map/all_to_all | solution.py:368
  64.2 5.3 %shard_map.111 = (bf16[192,2048]{1,0:T(8,128)(2,1)}, bf16[192,2048]{1,0:T(8,128)(2,1)}, bf16[192,1024]{1,0:T(8,128)(2,1)}, bf16[192,128]{1,0:T(8,128)(2,1)}, f32...) custom-call(s32[3]{0:T(128)S(1)} %pad_add_fusion.core_ref.place_ref, bf16[4992,128]{1,0:T(8,128)(2,1)S(1)} %bitcast.35, ...), custom_call_target="tpu_custom_call" | custom-call | flops 4000000000 | bytes 12000000 | tf_op jit(solution)/shard_map/pallas_call | solution.py:464
  69.7 8.4 %shard_map.113.back_in = bf16[4992,128]{1,0:T(8,128)(2,1)S(1)} custom-call(s32[3]{0:T(128)S(1)} %pad_add_fusion.core_ref.place_ref, bf16[192,2048]{1,0:T(8,128)(2,1)} %get-tuple-element.20.x_hbm, bf16[192,2048]{1,0:T(8,128)(2,1)} %get-tuple-element.17.mixed_hbm, bf16[192,1024]{1,0:T(8,128)(2,1)} %get-tuple-element.18.grad_hbm, ...), custom_call_target="tpu_custom_call" | custom-call | flops 7000000000 | bytes 21000000 | tf_op jit(solution)/shard_map/pallas_call | solution.py:477
  78.2 1.0 copy-done.1
  79.2 3.9 %shard_map.114 = (bf16[8,128,1024]{2,1,0:T(8,128)(2,1)}, bf16[4992,128]{1,0:T(8,128)(2,1)}) custom-call(s32[3]{0:T(128)S(1)} %pad_add_fusion.core_ref.place_ref, bf16[192,2048]{1,0:T(8,128)(2,1)} %get-tuple-element.17.mixed_hbm, bf16[192,1024]{1,0:T(8,128)(2,1)} %get-tuple-element.18.grad_hbm, ...), custom_call_target="tpu_custom_call", output_to_operand_aliasing={{1}: (4, {})} | custom-call | flops 2000000000 | bytes 6000000 | tf_op jit(solution)/shard_map/pallas_call | solution.py:489
  83.2 1.2 copy-done.2
  84.4 49.9 %all_to_all.15 = bf16[16,312,128]{2,1,0:T(8,128)(2,1)S(1)} all-to-all(bf16[16,312,128]{2,1,0:T(8,128)(2,1)S(1)} %bitcast.36), channel_id=1, replica_groups=mesh['clip'=16,'tm'=16] {'tm'}, dimensions={0} | all-to-all | bytes 2555904 | tf_op jit(solution)/shard_map/all_to_all | solution.py:368
  134.4 8.7 %shard_map.115 = (bf16[192,1024]{1,0:T(8,128)(2,1)}, bf16[192,2048]{1,0:T(8,128)(2,1)}, bf16[192,256]{1,0:T(8,128)(2,1)}, bf16[64,192]{1,0:T(8,128)(2,1)}) custom-call(bf16[192,2048]{1,0:T(8,128)(2,1)S(1)} %bitcast.39, bf16[4992,128]{1,0:T(8,128)(2,1)S(1)} %bitcast.37, bf16[192,256]{1,0:T(8,128)(2,1)S(1)} %bitcast.41, bf16[64,192]{1,0:T(8,128)(2,1)S(1)} %bitcast.43, ...), custom_call_target="tpu_custom_call" | custom-call | flops 8000000000 | bytes 24000000 | tf_op jit(solution)/shard_map/pallas_call | solution.py:504
  143.1 1.8 %bitcast_convert_fusion = f32[128,1024]{1,0:T(8,128)} fusion(bf16[1,128,1024]{2,1,0:T(8,128)(2,1)} %reduce-scatter.2.cloned.1.call-done), kind=kLoop, calls=%fused_computation.2 | loop fusion | flops 131072 | bytes 786432 | tf_op jit(solution)/shard_map/convert_element_type | solution.py:512
  (32 shorter events, 2.7 us)
Async XLA Ops:
  7.2 1.0 copy-start
  8.8 19.1 %all-to-all-start.1 = ((bf16[16,16,256]{2,1,0:T(8,128)(2,1)}), bf16[16,16,256]{2,1,0:T(8,128)(2,1)S(1)}, u32[]{:S(2)}, u32[]{:S(2)}) async-start(bf16[16,16,256]{2,1,0:T(8,128)(2,1)} %bitcast.12), calls=%async_computation.1 | async-start | bytes 262144 | tf_op jit(solution)/shard_map/all_to_all | solution.py:418
  18.8 0.7 copy-start.6
  27.9 3.7 %copy-start.9 = (bf16[16,16,256]{2,1,0:T(8,128)(2,1)}, bf16[16,16,256]{2,1,0:T(8,128)(2,1)S(1)}, u32[]{:S(2)}) copy-start(bf16[16,16,256]{2,1,0:T(8,128)(2,1)S(1)} %all-to-all-done.1.v_in) | copy-start | bytes 393220
  27.9 36.2 %all-to-all-start = ((bf16[16,312,128]{2,1,0:T(8,128)(2,1)}), bf16[16,312,128]{2,1,0:T(8,128)(2,1)S(1)}, u32[]{:S(2)}, u32[]{:S(2)}) async-start(bf16[16,312,128]{2,1,0:T(8,128)(2,1)} %bitcast.8), calls=%async_computation | async-start | bytes 2555904 | tf_op jit(solution)/shard_map/all_to_all | solution.py:368
  31.6 111.4 %reduce-scatter.2.cloned.1.call-start = ((), (), s32[]{:S(2)}) async-start(), calls=%async_computation.4 | async-start | bytes 2359296 | tf_op jit(solution)/shard_map/reduce_scatter | solution.py:499
  31.7 6.2 %collective-permute-start.3 = (bf16[16,16,256]{2,1,0:T(8,128)(2,1)}, bf16[16,16,256]{2,1,0:T(8,128)(2,1)S(1)}, u32[]{:S(2)}, u32[]{:S(2)}) collective-permute-start(bf16[16,16,256]{2,1,0:T(8,128)(2,1)} %shard_map.112), channel_id=1, source_target_pairs={{0,48},{1,193},{2,50},{3,195},{4,52},{5,197},{6,54},{7,199},{8,56}... | collective-permute-start | bytes 393224 | tf_op jit(solution)/shard_map/ppermute | solution.py:429
  34.3 5.8 %collective-permute-start.2 = (bf16[16,16,256]{2,1,0:T(8,128)(2,1)}, bf16[16,16,256]{2,1,0:T(8,128)(2,1)S(1)}, u32[]{:S(2)}, u32[]{:S(2)}) collective-permute-start(bf16[16,16,256]{2,1,0:T(8,128)(2,1)} %shard_map.112), channel_id=1, source_target_pairs={{0,32},{1,129},{2,34},{3,131},{4,36},{5,133},{6,38},{7,135},{8,40}... | collective-permute-start | bytes 393224 | tf_op jit(solution)/shard_map/ppermute | solution.py:429
  34.8 5.3 %collective-permute-start.1 = (bf16[16,16,256]{2,1,0:T(8,128)(2,1)}, bf16[16,16,256]{2,1,0:T(8,128)(2,1)S(1)}, u32[]{:S(2)}, u32[]{:S(2)}) collective-permute-start(bf16[16,16,256]{2,1,0:T(8,128)(2,1)} %shard_map.112), channel_id=1, source_target_pairs={{0,16},{1,65},{2,18},{3,67},{4,20},{5,69},{6,22},{7,71},{8,24},{9,... | collective-permute-start | bytes 393224 | tf_op jit(solution)/shard_map/ppermute | solution.py:429
  41.1 15.2 %collective-permute-start.6 = (bf16[4,16,16,256]{3,2,1,0:T(8,128)(2,1)S(1)}, bf16[4,16,16,256]{3,2,1,0:T(8,128)(2,1)S(1)}, u32[]{:S(2)}, u32[]{:S(2)}) collective-permute-start(bf16[4,16,16,256]{3,2,1,0:T(8,128)(2,1)S(1)} %get-tuple-element.30), channel_id=1, source_target_pairs={{0,192},{1,49},{2,194},{3,51},{4,196},{5,53},{6,198},{7,55},{8,200... | collective-permute-start | bytes 1572872 | tf_op jit(solution)/shard_map/ppermute | solution.py:429
  43.6 12.7 %collective-permute-start.5 = (bf16[4,16,16,256]{3,2,1,0:T(8,128)(2,1)S(1)}, bf16[4,16,16,256]{3,2,1,0:T(8,128)(2,1)S(1)}, u32[]{:S(2)}, u32[]{:S(2)}) collective-permute-start(bf16[4,16,16,256]{3,2,1,0:T(8,128)(2,1)S(1)} %get-tuple-element.30), channel_id=1, source_target_pairs={{0,128},{1,33},{2,130},{3,35},{4,132},{5,37},{6,134},{7,39},{8,136... | collective-permute-start | bytes 1572872 | tf_op jit(solution)/shard_map/ppermute | solution.py:429
  44.0 13.0 %collective-permute-start.4 = (bf16[4,16,16,256]{3,2,1,0:T(8,128)(2,1)S(1)}, bf16[4,16,16,256]{3,2,1,0:T(8,128)(2,1)S(1)}, u32[]{:S(2)}, u32[]{:S(2)}) collective-permute-start(bf16[4,16,16,256]{3,2,1,0:T(8,128)(2,1)S(1)} %get-tuple-element.30), channel_id=1, source_target_pairs={{0,64},{1,17},{2,66},{3,19},{4,68},{5,21},{6,70},{7,23},{8,72},{9,... | collective-permute-start | bytes 1572872 | tf_op jit(solution)/shard_map/ppermute | solution.py:429
  57.0 7.2 %copy-start.7 = (f32[2,32]{1,0:T(2,128)S(1)}, f32[2,32]{1,0:T(2,128)}, u32[]{:S(2)}) copy-start(f32[2,32]{1,0:T(2,128)} %rate_ref.7) | copy-start | bytes 772
  57.0 7.2 %copy-start.8 = (f32[32]{0:T(128)S(1)}, f32[32]{0:T(128)}, u32[]{:S(2)}) copy-start(f32[32]{0:T(128)} %param.11) | copy-start | bytes 388
  58.5 11.2 %collective-permute-start.7 = (bf16[4,4,16,16,256]{4,3,2,1,0:T(8,128)(2,1)}, bf16[4,4,16,16,256]{4,3,2,1,0:T(8,128)(2,1)}, u32[]{:S(2)}, u32[]{:S(2)}) collective-permute-start(bf16[4,4,16,16,256]{4,3,2,1,0:T(8,128)(2,1)} %pad_maximum_fusion.mine_hbm), channel_id=1, source_target_pairs={{0,1},{1,0},{2,3},{3,2},{4,5},{5,4},{6,7},{7,6},{8,9},{9,8},{10,11... | collective-permute-start | bytes 6291464 | tf_op jit(solution)/shard_map/ppermute | solution.py:392
  69.4 9.8 %collective-permute-start = (bf16[8,128,1024]{2,1,0:T(8,128)(2,1)}, bf16[8,128,1024]{2,1,0:T(8,128)(2,1)S(1)}, u32[]{:S(2)}, u32[]{:S(2)}) collective-permute-start(bf16[8,128,1024]{2,1,0:T(8,128)(2,1)} %get-tuple-element.19), channel_id=1, source_target_pairs={{0,1},{1,0},{2,3},{3,2},{4,5},{5,4},{6,7},{7,6},{8,9},{9,8},{10,11... | collective-permute-start | bytes 6291464 | tf_op jit(solution)/shard_map/ppermute | solution.py:392
  78.1 1.1 copy-start.1
  83.1 1.3 copy-start.2
  83.2 51.2 %copy-start.3 = (bf16[1,192,2048]{2,1,0:T(8,128)(2,1)S(1)}, bf16[1,192,2048]{2,1,0:T(8,128)(2,1)}, u32[]{:S(2)}) copy-start(bf16[1,192,2048]{2,1,0:T(8,128)(2,1)} %param.7) | copy-start | bytes 2359300
  83.2 51.2 %copy-start.4 = (bf16[1,192,256]{2,1,0:T(8,128)(2,1)S(1)}, bf16[1,192,256]{2,1,0:T(8,128)(2,1)}, u32[]{:S(2)}) copy-start(bf16[1,192,256]{2,1,0:T(8,128)(2,1)} %param.8) | copy-start | bytes 294916
  83.2 51.2 %copy-start.5 = (bf16[1,192,64]{1,2,0:T(8,128)(2,1)S(1)}, bf16[1,192,64]{1,2,0:T(8,128)(2,1)}, u32[]{:S(2)}) copy-start(bf16[1,192,64]{1,2,0:T(8,128)(2,1)} %param.9) | copy-start | bytes 73732
Sparse Core Ops, SparseCore 0:
  83.3 58.2 reduce-scatter.1

commit v2 on v1

--- a/solution.py
+++ b/solution.py
@@ -91,7 +91,9 @@
     return pick_heads(dot(both_heads(pair, weights), x_pair))
 
 
-def scan_backward(blocks, gram_t, cum_row, from_col, x_pair, dy_pair, pair, dgram, rowsum, colsum):
+def scan_backward(
+    blocks, gram_t, cum_row, from_col, x_pair, dy_pair, pair, dgram, rowsum, colsum=None, by_x=None
+):
     products = dot(jnp.concatenate(split_pair(x_pair), axis=0), dy_pair, ((1,), (1,)))
     added = [None] * len(blocks)
 
@@ -101,14 +103,18 @@
         for n, ((j0, j1), (i0, i1)) in enumerate(blocks):
             e = jnp.exp2(jnp.minimum(from_col[j0:j1, h : h + 1] + cum_row[h : h + 1, i0:i1], CAP))
             w = e * gram_t[j0:j1, i0:i1]
+            rounded = w.astype(BF16)
+            if colsum is None:
+                w = rounded.astype(F32)
             base = ROWS * (h - 2 * pair)
             p = products[base + j0 : base + j1, i0:i1]
             t = p * e
             added[n] = t if added[n] is None else added[n] + t
             m = p * w
-            colsum[j0:j1, h : h + 1] = jnp.sum(m, axis=1, keepdims=True)
+            if colsum is not None:
+                colsum[j0:j1, h : h + 1] = jnp.sum(m, axis=1, keepdims=True)
             sums.append((i0, i1, jnp.sum(m, axis=0, keepdims=True)))
-            parts.append(w.astype(BF16))
+            parts.append(rounded)
         (a0, a1, first), (b0, b1, second) = sums
         if b0 < a1:
             rowsum[h : h + 1, a0:b0] = first[:, : b0 - a0]
@@ -119,16 +125,27 @@
         return padded(parts, blocks, ROWS)
 
     dx = pick_heads(dot(both_heads(pair, weights), dy_pair))
+    if colsum is None:
+        by_x[:, 128 * pair : 128 * pair + 128] = dx * x_pair.astype(F32)
     for ((j0, j1), (i0, i1)), t in zip(blocks, added):
         dgram[j0:j1, i0:i1] += t
     return dx
 
 
-def finish_backward(temporal, dgram, rowsum, colsum, b, c, raw, step, rate):
+def head_sums(v):
+    lane = lax.broadcasted_iota(jnp.int32, (2048, 128), 0)
+    head = lax.broadcasted_iota(jnp.int32, (2048, 128), 1)
+    ones = ((lane >> 6) == head).astype(BF16)
+    high = v.astype(BF16)
+    rest = (v - high.astype(F32)).astype(BF16)
+    both = dot(jnp.concatenate([high, rest], axis=0), ones)
+    return (both[:ROWS] + both[ROWS:])[:, :HEADS]
+
+
+def finish_backward(temporal, dgram, rowsum, col, b, c, raw, step, rate):
     dg = jnp.where(mask_of(temporal, True), dgram[...], 0.0).astype(BF16)
     db = dot(dg, c)
     dc = dot(dg, b, ((0,), (0,)))
-    col = colsum[...]
     dcum = rowsum[...].T - col
     dlog = dot(mask_of(temporal, True).astype(F32), dcum, precision=HIGH)
     dstep = col / step - rate * dlog
@@ -228,20 +245,22 @@
         y = scan_forward(TEMPORAL, gram, cum, from_row, xb, g)
         gain = jnp.where(low, gain_ref[0, 2 * g], gain_ref[0, 2 * g + 1])
         mixed_ref[:, 128 * g : 128 * g + 128] = (y + gain * x).astype(BF16)
-    save(x_ref, x_out)
-    save(mixed_ref, mixed_out)
+        if g % 4 == 3:
+            at = pl.ds(128 * (g - 3), 512)
+            save(x_ref.at[:, at], x_out.at[:, at])
+            save(mixed_ref.at[:, at], mixed_out.at[:, at])
     for column in range(0, MODEL, 256):
         dw = weight_grad(mixed_ref, grad_ref, 1 - core_ref[0], column)
-        other_ref[:, :, column : column + 256] = dw.reshape(8, 128, 256).astype(BF16)
-    save(other_ref, other_out)
+        at = pl.ds(column, 256)
+        other_ref[:, :, at] = dw.reshape(8, 128, 256).astype(BF16)
+        save(other_ref.at[:, :, at], other_out.at[:, :, at])
     for copy in saves:
         copy.wait()
 
 
 def weight_grad_kernel(
-    core_ref, mixed_hbm, grad_hbm, got_ref, back_in, out_ref, back_out, mixed_ref, grad_ref, sems
+    core_ref, mixed_hbm, grad_hbm, got_ref, out_hbm, mixed_ref, grad_ref, out_ref, sems
 ):
-    del back_in, back_out
     loads = [
         pltpu.make_async_copy(mixed_hbm, mixed_ref, sems.at[0]),
         pltpu.make_async_copy(grad_hbm, grad_ref, sems.at[1]),
@@ -250,10 +269,15 @@
         copy.start()
     for copy in loads:
         copy.wait()
-    for column in range(0, MODEL, 256):
-        at = slice(column, column + 256)
-        dw = weight_grad(mixed_ref, grad_ref, core_ref[0], column).reshape(8, 128, 256)
+    saves = []
+    for n in range(MODEL // 256):
+        at = pl.ds(256 * n, 256)
+        dw = weight_grad(mixed_ref, grad_ref, core_ref[0], 256 * n).reshape(8, 128, 256)
         out_ref[:, :, at] = (dw + got_ref[:, :, at].astype(F32)).astype(BF16)
+        saves.append(pltpu.make_async_copy(out_ref.at[:, :, at], out_hbm.at[:, :, at], sems.at[2 + n]))
+        saves[-1].start()
+    for copy in saves:
+        copy.wait()
 
 
 def temporal_backward_kernel(
@@ -302,7 +326,7 @@
         )
         gain = jnp.where(low, gain_ref[0, 2 * g], gain_ref[0, 2 * g + 1])
         put_temporal(wide, g, dx + gain * dy.astype(F32))
-    dbc, draw = finish_backward(True, dgram, rowsum, colsum, b, c, raw, step, rate)
+    dbc, draw = finish_backward(True, dgram, rowsum, colsum[...], b, c, raw, step, rate)
     put_temporal(wide, PAIRS + TILES, dbc)
     put_temporal(
         wide, PAIRS + TILES + 1, jnp.concatenate([draw, jnp.zeros((ROWS, 128 - HEADS), F32)], axis=1)
@@ -317,7 +341,7 @@
 
 def spatial_backward_kernel(
     x_ref, back_ref, bc_ref, raw_ref, rate_ref, out_ref, dx_ref, dbc_ref, draw_ref,
-    wide, dgram, rowsum, colsum,
+    wide, dgram, rowsum, by_x,
 ):
     wide[...] = back_ref[...].astype(F32)
     for k in range(TILES):
@@ -333,10 +357,10 @@
         dy = get_spatial(wide, g).astype(BF16)
         dx = scan_backward(
             SPATIAL_BWD, gram_t, cum_row, from_col, x_ref[:, 128 * g : 128 * g + 128], dy, g,
-            dgram, rowsum, colsum,
+            dgram, rowsum, by_x=by_x,
         )
         dx_ref[:, 128 * g : 128 * g + 128] = dx.astype(BF16)
-    dbc, draw = finish_backward(False, dgram, rowsum, colsum, b, c, raw, step, rate)
+    dbc, draw = finish_backward(False, dgram, rowsum, head_sums(by_x[...]), b, c, raw, step, rate)
     dbc_ref[:, 0:128] = dbc.astype(BF16)
     dbc_ref[:, 128:256] = get_spatial(wide, PAIRS + TILES).astype(BF16)
     draw_t = get_spatial(wide, PAIRS + TILES + 1)
@@ -467,13 +491,32 @@
         [smem()] + vmem(2) + [smem()],
         [wide]
         + [pltpu.VMEM(dims, dtype) for dims, dtype in zip(kept, types)]
-        + [pltpu.SemaphoreType.DMA((6,))],
+        + [pltpu.SemaphoreType.DMA((15,))],
         4,
         20,
         out_specs=hbm(6),
     )(core, ahead, decay_rate, gain)
 
     got = across("tm", other, 1)
+    partial = call(
+        weight_grad_kernel,
+        (pltpu.HBM((8, 128, MODEL), BF16),),
+        [smem()] + hbm(2) + vmem(1),
+        [
+            pltpu.VMEM((ROWS, 2048), BF16),
+            pltpu.VMEM((ROWS, MODEL), BF16),
+            pltpu.VMEM((8, 128, MODEL), BF16),
+            pltpu.SemaphoreType.DMA((6,)),
+        ],
+        3,
+        14,
+        out_specs=hbm(1),
+    )(core, *in_hbm(mixed, grad_t), got)[0]
+    grad_w = lax.psum_scatter(
+        partial, "tm", scatter_dimension=0, axis_index_groups=along_z, tiled=False
+    )
+    raw_t = after(raw_t, partial)
+
     back = call(
         temporal_backward_kernel,
         shape(ROWS * SENT, 128),
@@ -485,27 +528,13 @@
         7,
         24,
     )(core, *in_hbm(x_t, mixed, grad_t, bc_t, raw_t, mine, theirs), decay_rate, gain)
-
-    partial, back = call(
-        weight_grad_kernel,
-        (shape(8, 128, MODEL), pltpu.HBM((ROWS * SENT, 128), BF16)),
-        [smem()] + hbm(2) + vmem(1) + hbm(1),
-        [pltpu.VMEM((ROWS, 2048), BF16), pltpu.VMEM((ROWS, MODEL), BF16), pltpu.SemaphoreType.DMA((2,))],
-        2,
-        14,
-        out_specs=vmem(1) + hbm(1),
-        aliases={4: 1},
-    )(core, *in_hbm(mixed, grad_t), got, *in_hbm(back))
-    grad_w = lax.psum_scatter(
-        partial, "tm", scatter_dimension=0, axis_index_groups=along_z, tiled=False
-    )
     back = exchange(back)
 
     mixed_out, grad_x, grad_bc, grad_step = call(
         spatial_backward_kernel,
         (shape(ROWS, MODEL), shape(ROWS, 2048), shape(ROWS, 256), shape(2 * HEADS, ROWS)),
         vmem(5),
-        [wide] + scan_scratch(),
+        [wide] + scan_scratch()[:2] + [pltpu.VMEM((ROWS, 2048), F32)],
         8,
         18,
     )(x, back, bc, raw, decay_rate)

time: 152 us -> 150 us (0.987)
  waiting for transfers between devices: 24.1 us -> 29.3 us
  Pallas kernels: 31.2 us -> 27.5 us
  starting transfers between devices: 23.3 us -> 21 us
  blocking collectives: 49.9 us -> 47.7 us
    all_to_all x1, waiting for transfers between devices: 2.94 us -> 19.7 us  [exchange(): return lax.all_to_all(blocks, 'tm', 0, 0, tiled=True).reshape(v.shape)]
    ppermute x6, waiting for transfers between devices: 17.6 us -> 4.99 us  [gather_weight(): got.append(lax.ppermute(part, ('clip', 'tm'), to))]
    pallas_call x1, Pallas kernels: 8.67 us -> 5.47 us  [on_device(): call(spatial_backward_kernel, (shape(ROWS, MODEL), shape(ROWS, 2048), sha...]
    ppermute x2, starting transfers between devices: 2.91 us -> 0.57 us  [across(): return lax.ppermute(v, axis, [(s, s ^ bit) for s in range(16)])]
    all_to_all x1, blocking collectives: 49.9 us -> 47.7 us  [exchange(): return lax.all_to_all(blocks, 'tm', 0, 0, tiled=True).reshape(v.shape)]
    unnamed x20 -> x18, local copies, waits for them, and re-layouts: 3.91 us -> 2.95 us
  transfers between devices with their start and end apart: 11 -> 11, of which waited for: 6 -> 5; matrix products, arithmetic and copies ran while one was open for 2% -> 3% of each run, Pallas kernels for 18% -> 18%
where the time goes in v2:
time: 150 us; the launch traced here: 149 us
  blocking collectives  47.7 us (32%)
  waiting for transfers between devices  29.3 us (20%)
  Pallas kernels  27.5 us (18%)
  starting transfers between devices  21 us (14%)
  between operations  14.2 us (9%)
  other arithmetic  5.66 us (4%)
  local copies, waits for them, and re-layouts  3.62 us (2%)
    all_to_all x1, blocking collectives, exchange(): return lax.all_to_all(blocks, 'tm', 0, 0, tiled=True).reshape(v.shape)  47.7 us
    all_to_all x1, waiting for transfers between devices, exchange(): return lax.all_to_all(blocks, 'tm', 0, 0, tiled=True).reshape(v.shape)  19.7 us
    all_to_all x1, starting transfers between devices, weight_part(): return lax.all_to_all(jnp.tile(mine, (8, 1, 1)), 'tm', 0, 0, tiled=True)  9.98 us
    pallas_call x1, Pallas kernels, on_device(): call(temporal_backward_kernel, shape(ROWS * SENT, 128), [smem()] + hbm(7)...  8.39 us
    ppermute x6, starting transfers between devices, gather_weight(): got.append(lax.ppermute(part, ('clip', 'tm'), to))  6.68 us
    pallas_call x1, Pallas kernels, on_device(): call(spatial_backward_kernel, (shape(ROWS, MODEL), shape(ROWS, 2048), sha...  5.47 us
    pallas_call x1, Pallas kernels, on_device(): call(temporal_forward_kernel, tuple((pltpu.HBM(dims, dtype) for dims, dty...  5.02 us
    ppermute x6, waiting for transfers between devices, gather_weight(): got.append(lax.ppermute(part, ('clip', 'tm'), to))  4.99 us
  transfers between devices with their start and end apart: 11, of which 5 were waited for; matrix products, arithmetic and copies ran while one was open for 3% of the time, Pallas kernels for 18%

profile of v2, /device:TPU:1, one launch (start us, length us, event | category | flops | bytes accessed | tf_op | source)
XLA Modules:
  0.0 149.1 jit_solution(7140774379426599429)
XLA Ops:
  7.2 0.9 copy-done
  8.1 0.7 tile.4
  8.8 10.0 %all-to-all-start.1 = ((bf16[16,16,256]{2,1,0:T(8,128)(2,1)}), bf16[16,16,256]{2,1,0:T(8,128)(2,1)S(1)}, u32[]{:S(2)}, u32[]{:S(2)}) async-start(bf16[16,16,256]{2,1,0:T(8,128)(2,1)} %bitcast.12), calls=%async_computation.1 | async-start | bytes 262144 | tf_op jit(solution)/shard_map/all_to_all | solution.py:442
  18.8 0.7 copy-done.4
  19.5 4.9 %shard_map.110.token = bf16[4992,128]{1,0:T(8,128)(2,1)} custom-call(bf16[192,2048]{1,0:T(8,128)(2,1)} %bitcast.38, bf16[192,256]{1,0:T(8,128)(2,1)} %bitcast.40, bf16[64,192]{1,0:T(8,128)(2,1)} %bitcast.42, bf16[192,1024]{1,0:T(8,128)(2,1)} %bitcast.51, f32[2,32]{1,0:T(2,128)S(1)} %copy-done.4), custom_call_target="tpu_custom_call" | custom-call | flops 4000000000 | bytes 12000000 | tf_op jit(solution)/shard_map/pallas_call | solution.py:468
  24.4 3.6 %all-to-all-done.1.v_in = bf16[16,16,256]{2,1,0:T(8,128)(2,1)S(1)} async-done(((bf16[16,16,256]{2,1,0:T(8,128)(2,1)}), bf16[16,16,256]{2,1,0:T(8,128)(2,1)S(1)}, u32[]{:S(2)}, u32[]{:S(2)}) %all-to-all-start.1) | async-done | bytes 131104 | tf_op jit(solution)/shard_map/all_to_all | solution.py:442
  27.9 3.7 %all-to-all-start = ((bf16[16,312,128]{2,1,0:T(8,128)(2,1)}), bf16[16,312,128]{2,1,0:T(8,128)(2,1)S(1)}, u32[]{:S(2)}, u32[]{:S(2)}) async-start(bf16[16,312,128]{2,1,0:T(8,128)(2,1)} %bitcast.8), calls=%async_computation | async-start | bytes 2555904 | tf_op jit(solution)/shard_map/all_to_all | solution.py:392
  31.7 2.6 %collective-permute-start.3 = (bf16[16,16,256]{2,1,0:T(8,128)(2,1)}, bf16[16,16,256]{2,1,0:T(8,128)(2,1)S(1)}, u32[]{:S(2)}, u32[]{:S(2)}) collective-permute-start(bf16[16,16,256]{2,1,0:T(8,128)(2,1)} %shard_map.114), channel_id=1, source_target_pairs={{0,48},{1,193},{2,50},{3,195},{4,52},{5,197},{6,54},{7,199},{8,56}... | collective-permute-start | bytes 393224 | tf_op jit(solution)/shard_map/ppermute | solution.py:453
  34.3 0.5 collective-permute-start.2
  35.2 2.8 %collective-permute-done.3 = bf16[16,16,256]{2,1,0:T(8,128)(2,1)S(1)} collective-permute-done((bf16[16,16,256]{2,1,0:T(8,128)(2,1)}, bf16[16,16,256]{2,1,0:T(8,128)(2,1)S(1)}, u32[]{:S(2)}, u32[]{:S(2)}) %collective-permute-start.3) | collective-permute-done | bytes 131104 | tf_op jit(solution)/shard_map/ppermute | solution.py:453
  38.0 2.2 %collective-permute-done.2 = bf16[16,16,256]{2,1,0:T(8,128)(2,1)S(1)} collective-permute-done((bf16[16,16,256]{2,1,0:T(8,128)(2,1)}, bf16[16,16,256]{2,1,0:T(8,128)(2,1)S(1)}, u32[]{:S(2)}, u32[]{:S(2)}) %collective-permute-start.2) | collective-permute-done | bytes 131104 | tf_op jit(solution)/shard_map/ppermute | solution.py:453
  40.1 1.0 fusion
  41.1 2.5 %collective-permute-start.6 = (bf16[4,16,16,256]{3,2,1,0:T(8,128)(2,1)S(1)}, bf16[4,16,16,256]{3,2,1,0:T(8,128)(2,1)S(1)}, u32[]{:S(2)}, u32[]{:S(2)}) collective-permute-start(bf16[4,16,16,256]{3,2,1,0:T(8,128)(2,1)S(1)} %get-tuple-element.26), channel_id=1, source_target_pairs={{0,192},{1,49},{2,194},{3,51},{4,196},{5,53},{6,198},{7,55},{8,200... | collective-permute-start | bytes 1572872 | tf_op jit(solution)/shard_map/ppermute | solution.py:453
  44.5 19.7 %all-to-all-done = bf16[16,312,128]{2,1,0:T(8,128)(2,1)S(1)} async-done(((bf16[16,312,128]{2,1,0:T(8,128)(2,1)}), bf16[16,312,128]{2,1,0:T(8,128)(2,1)S(1)}, u32[]{:S(2)}, u32[]{:S(2)}) %all-to-all-start) | async-done | bytes 1277984 | tf_op jit(solution)/shard_map/all_to_all | solution.py:392
  64.2 5.0 %shard_map.111 = (bf16[192,2048]{1,0:T(8,128)(2,1)}, bf16[192,2048]{1,0:T(8,128)(2,1)}, bf16[192,1024]{1,0:T(8,128)(2,1)}, bf16[192,128]{1,0:T(8,128)(2,1)}, f32...) custom-call(s32[3]{0:T(128)S(1)} %pad_add_fusion.core_ref.place_ref, bf16[4992,128]{1,0:T(8,128)(2,1)S(1)} %bitcast.35, ...), custom_call_target="tpu_custom_call" | custom-call | flops 4000000000 | bytes 12000000 | tf_op jit(solution)/shard_map/pallas_call | solution.py:488
  69.3 2.8 %pad_maximum_fusion.mine_hbm = bf16[4,4,16,16,256]{4,3,2,1,0:T(8,128)(2,1)} fusion(bf16[1,4,16,16,256]{4,3,2,1,0:T(8,128)(2,1)S(1)} %bitcast.47, bf16[1,4,16,16,256]{4,3,2,1,0:T(8,128)(2,1)} %bitcast.19, bf16[1,4,16,16,256]{4,3,2,1,0:T(8,128)(2,1)} %bitcast.18, bf16[1,4,16,16,256]{4,3,2,1,0:T(8,128)(2,1)S(1)} %get-tuple-element.25), kind=kLoop, calls=%fused_computation | loop fusion | flops 3145728 | bytes 4194304 | tf_op jit(solution)/shard_map/stack | solution.py:454
  72.2 0.5 collective-permute-start.7
  72.6 1.0 collective-permute-done.got_ref
  73.7 3.7 %shard_map.112.token = bf16[8,128,1024]{2,1,0:T(8,128)(2,1)} custom-call(s32[3]{0:T(128)S(1)} %pad_add_fusion.core_ref.place_ref, bf16[192,2048]{1,0:T(8,128)(2,1)} %get-tuple-element.16.mixed_hbm, bf16[192,1024]{1,0:T(8,128)(2,1)} %get-tuple-element.17.grad_hbm, bf16[8,128,1024]{2,1,0:T(8,128)(2,1)S(1)} %collective-permute-done.got_ref), custom_call_target="tpu_custom_call" | custom-call | flops 3000000000 | bytes 9000000 | tf_op jit(solution)/shard_map/pallas_call | solution.py:501
  77.5 1.3 copy-done.8
  78.8 8.4 %shard_map.115 = bf16[4992,128]{1,0:T(8,128)(2,1)S(1)} custom-call(s32[3]{0:T(128)S(1)} %pad_add_fusion.core_ref.place_ref, bf16[192,2048]{1,0:T(8,128)(2,1)} %get-tuple-element.15.x_hbm, bf16[192,2048]{1,0:T(8,128)(2,1)} %get-tuple-element.16.mixed_hbm, bf16[192,1024]{1,0:T(8,128)(2,1)} %get-tuple-element.17.grad_hbm, ...), custom_call_target="tpu_custom_call" | custom-call | flops 7000000000 | bytes 21000000 | tf_op jit(solution)/shard_map/pallas_call | solution.py:520
  87.2 47.7 %all_to_all.15 = bf16[16,312,128]{2,1,0:T(8,128)(2,1)S(1)} all-to-all(bf16[16,312,128]{2,1,0:T(8,128)(2,1)S(1)} %bitcast.36), channel_id=1, replica_groups=mesh['clip'=16,'tm'=16] {'tm'}, dimensions={0} | all-to-all | bytes 2555904 | tf_op jit(solution)/shard_map/all_to_all | solution.py:392
  135.0 5.5 %shard_map.116 = (bf16[192,1024]{1,0:T(8,128)(2,1)}, bf16[192,2048]{1,0:T(8,128)(2,1)}, bf16[192,256]{1,0:T(8,128)(2,1)}, bf16[64,192]{1,0:T(8,128)(2,1)}) custom-call(bf16[192,2048]{1,0:T(8,128)(2,1)S(1)} %bitcast.39, bf16[4992,128]{1,0:T(8,128)(2,1)S(1)} %bitcast.37, bf16[192,256]{1,0:T(8,128)(2,1)S(1)} %bitcast.41, bf16[64,192]{1,0:T(8,128)(2,1)S(1)} %bitcast.43, ...), custom_call_target="tpu_custom_call" | custom-call | flops 8000000000 | bytes 24000000 | tf_op jit(solution)/shard_map/pallas_call | solution.py:533
  140.4 1.8 %bitcast_convert_fusion = f32[128,1024]{1,0:T(8,128)} fusion(bf16[1,128,1024]{2,1,0:T(8,128)(2,1)} %reduce-scatter.2.cloned.1.call-done), kind=kLoop, calls=%fused_computation.2 | loop fusion | flops 131072 | bytes 786432 | tf_op jit(solution)/shard_map/convert_element_type | solution.py:541
  (31 shorter events, 1.4 us)
Async XLA Ops:
  7.2 1.0 copy-start
  8.8 19.1 %all-to-all-start.1 = ((bf16[16,16,256]{2,1,0:T(8,128)(2,1)}), bf16[16,16,256]{2,1,0:T(8,128)(2,1)S(1)}, u32[]{:S(2)}, u32[]{:S(2)}) async-start(bf16[16,16,256]{2,1,0:T(8,128)(2,1)} %bitcast.12), calls=%async_computation.1 | async-start | bytes 262144 | tf_op jit(solution)/shard_map/all_to_all | solution.py:442
  18.8 0.7 copy-start.4
  27.9 3.8 %copy-start.7 = (bf16[16,16,256]{2,1,0:T(8,128)(2,1)}, bf16[16,16,256]{2,1,0:T(8,128)(2,1)S(1)}, u32[]{:S(2)}) copy-start(bf16[16,16,256]{2,1,0:T(8,128)(2,1)S(1)} %all-to-all-done.1.v_in) | copy-start | bytes 393220
  27.9 36.2 %all-to-all-start = ((bf16[16,312,128]{2,1,0:T(8,128)(2,1)}), bf16[16,312,128]{2,1,0:T(8,128)(2,1)S(1)}, u32[]{:S(2)}, u32[]{:S(2)}) async-start(bf16[16,312,128]{2,1,0:T(8,128)(2,1)} %bitcast.8), calls=%async_computation | async-start | bytes 2555904 | tf_op jit(solution)/shard_map/all_to_all | solution.py:392
  31.6 32.5 %copy-start.5 = (f32[2,32]{1,0:T(2,128)S(1)}, f32[2,32]{1,0:T(2,128)}, u32[]{:S(2)}) copy-start(f32[2,32]{1,0:T(2,128)} %rate_ref.7) | copy-start | bytes 772
  31.6 32.5 %copy-start.6 = (f32[32]{0:T(128)S(1)}, f32[32]{0:T(128)}, u32[]{:S(2)}) copy-start(f32[32]{0:T(128)} %param.11) | copy-start | bytes 388
  31.7 108.8 %reduce-scatter.2.cloned.1.call-start = ((), (), s32[]{:S(2)}) async-start(), calls=%async_computation.4 | async-start | bytes 2359296 | tf_op jit(solution)/shard_map/reduce_scatter | solution.py:515
  31.7 6.2 %collective-permute-start.3 = (bf16[16,16,256]{2,1,0:T(8,128)(2,1)}, bf16[16,16,256]{2,1,0:T(8,128)(2,1)S(1)}, u32[]{:S(2)}, u32[]{:S(2)}) collective-permute-start(bf16[16,16,256]{2,1,0:T(8,128)(2,1)} %shard_map.114), channel_id=1, source_target_pairs={{0,48},{1,193},{2,50},{3,195},{4,52},{5,197},{6,54},{7,199},{8,56}... | collective-permute-start | bytes 393224 | tf_op jit(solution)/shard_map/ppermute | solution.py:453
  34.3 5.8 %collective-permute-start.2 = (bf16[16,16,256]{2,1,0:T(8,128)(2,1)}, bf16[16,16,256]{2,1,0:T(8,128)(2,1)S(1)}, u32[]{:S(2)}, u32[]{:S(2)}) collective-permute-start(bf16[16,16,256]{2,1,0:T(8,128)(2,1)} %shard_map.114), channel_id=1, source_target_pairs={{0,32},{1,129},{2,34},{3,131},{4,36},{5,133},{6,38},{7,135},{8,40}... | collective-permute-start | bytes 393224 | tf_op jit(solution)/shard_map/ppermute | solution.py:453
  34.8 5.3 %collective-permute-start.1 = (bf16[16,16,256]{2,1,0:T(8,128)(2,1)}, bf16[16,16,256]{2,1,0:T(8,128)(2,1)S(1)}, u32[]{:S(2)}, u32[]{:S(2)}) collective-permute-start(bf16[16,16,256]{2,1,0:T(8,128)(2,1)} %shard_map.114), channel_id=1, source_target_pairs={{0,16},{1,65},{2,18},{3,67},{4,20},{5,69},{6,22},{7,71},{8,24},{9,... | collective-permute-start | bytes 393224 | tf_op jit(solution)/shard_map/ppermute | solution.py:453
  41.1 28.2 %collective-permute-start.6 = (bf16[4,16,16,256]{3,2,1,0:T(8,128)(2,1)S(1)}, bf16[4,16,16,256]{3,2,1,0:T(8,128)(2,1)S(1)}, u32[]{:S(2)}, u32[]{:S(2)}) collective-permute-start(bf16[4,16,16,256]{3,2,1,0:T(8,128)(2,1)S(1)} %get-tuple-element.26), channel_id=1, source_target_pairs={{0,192},{1,49},{2,194},{3,51},{4,196},{5,53},{6,198},{7,55},{8,200... | collective-permute-start | bytes 1572872 | tf_op jit(solution)/shard_map/ppermute | solution.py:453
  43.7 25.7 %collective-permute-start.5 = (bf16[4,16,16,256]{3,2,1,0:T(8,128)(2,1)S(1)}, bf16[4,16,16,256]{3,2,1,0:T(8,128)(2,1)}, u32[]{:S(2)}, u32[]{:S(2)}) collective-permute-start(bf16[4,16,16,256]{3,2,1,0:T(8,128)(2,1)S(1)} %get-tuple-element.26), channel_id=1, source_target_pairs={{0,128},{1,33},{2,130},{3,35},{4,132},{5,37},{6,134},{7,39},{8,136... | collective-permute-start | bytes 1572872 | tf_op jit(solution)/shard_map/ppermute | solution.py:453
  44.0 25.3 %collective-permute-start.4 = (bf16[4,16,16,256]{3,2,1,0:T(8,128)(2,1)S(1)}, bf16[4,16,16,256]{3,2,1,0:T(8,128)(2,1)}, u32[]{:S(2)}, u32[]{:S(2)}) collective-permute-start(bf16[4,16,16,256]{3,2,1,0:T(8,128)(2,1)S(1)} %get-tuple-element.26), channel_id=1, source_target_pairs={{0,64},{1,17},{2,66},{3,19},{4,68},{5,21},{6,70},{7,23},{8,72},{9,... | collective-permute-start | bytes 1572872 | tf_op jit(solution)/shard_map/ppermute | solution.py:453
  69.2 4.5 %collective-permute-start = (bf16[8,128,1024]{2,1,0:T(8,128)(2,1)}, bf16[8,128,1024]{2,1,0:T(8,128)(2,1)S(1)}, u32[]{:S(2)}, u32[]{:S(2)}) collective-permute-start(bf16[8,128,1024]{2,1,0:T(8,128)(2,1)} %get-tuple-element.20), channel_id=1, source_target_pairs={{0,1},{1,0},{2,3},{3,2},{4,5},{5,4},{6,7},{7,6},{8,9},{9,8},{10,11... | collective-permute-start | bytes 6291464 | tf_op jit(solution)/shard_map/ppermute | solution.py:416
  72.2 5.3 %collective-permute-start.7 = (bf16[4,4,16,16,256]{4,3,2,1,0:T(8,128)(2,1)}, bf16[4,4,16,16,256]{4,3,2,1,0:T(8,128)(2,1)S(1)}, u32[]{:S(2)}, u32[]{:S(2)}) collective-permute-start(bf16[4,4,16,16,256]{4,3,2,1,0:T(8,128)(2,1)} %pad_maximum_fusion.mine_hbm), channel_id=1, source_target_pairs={{0,1},{1,0},{2,3},{3,2},{4,5},{5,4},{6,7},{7,6},{8,9},{9,8},{10,11... | collective-permute-start | bytes 6291464 | tf_op jit(solution)/shard_map/ppermute | solution.py:416
  77.4 1.3 copy-start.8
  87.2 47.8 %copy-start.1 = (bf16[1,192,2048]{2,1,0:T(8,128)(2,1)S(1)}, bf16[1,192,2048]{2,1,0:T(8,128)(2,1)}, u32[]{:S(2)}) copy-start(bf16[1,192,2048]{2,1,0:T(8,128)(2,1)} %param.7) | copy-start | bytes 2359300
  87.2 47.8 %copy-start.2 = (bf16[1,192,256]{2,1,0:T(8,128)(2,1)S(1)}, bf16[1,192,256]{2,1,0:T(8,128)(2,1)}, u32[]{:S(2)}) copy-start(bf16[1,192,256]{2,1,0:T(8,128)(2,1)} %param.8) | copy-start | bytes 294916
  87.2 47.7 %copy-start.3 = (bf16[1,192,64]{1,2,0:T(8,128)(2,1)S(1)}, bf16[1,192,64]{1,2,0:T(8,128)(2,1)}, u32[]{:S(2)}) copy-start(bf16[1,192,64]{1,2,0:T(8,128)(2,1)} %param.9) | copy-start | bytes 73732
Sparse Core Ops, SparseCore 0:
  77.5 60.4 reduce-scatter.1

commit v3 on v2

--- a/solution.py
+++ b/solution.py
@@ -259,22 +259,14 @@
 
 
 def weight_grad_kernel(
-    core_ref, mixed_hbm, grad_hbm, got_ref, out_hbm, mixed_ref, grad_ref, out_ref, sems
+    core_ref, mixed_ref, grad_ref, got_ref, out_hbm, out_ref, sems
 ):
-    loads = [
-        pltpu.make_async_copy(mixed_hbm, mixed_ref, sems.at[0]),
-        pltpu.make_async_copy(grad_hbm, grad_ref, sems.at[1]),
-    ]
-    for copy in loads:
-        copy.start()
-    for copy in loads:
-        copy.wait()
     saves = []
     for n in range(MODEL // 256):
         at = pl.ds(256 * n, 256)
         dw = weight_grad(mixed_ref, grad_ref, core_ref[0], 256 * n).reshape(8, 128, 256)
         out_ref[:, :, at] = (dw + got_ref[:, :, at].astype(F32)).astype(BF16)
-        saves.append(pltpu.make_async_copy(out_ref.at[:, :, at], out_hbm.at[:, :, at], sems.at[2 + n]))
+        saves.append(pltpu.make_async_copy(out_ref.at[:, :, at], out_hbm.at[:, :, at], sems.at[n]))
         saves[-1].start()
     for copy in saves:
         copy.wait()
@@ -501,17 +493,12 @@
     partial = call(
         weight_grad_kernel,
         (pltpu.HBM((8, 128, MODEL), BF16),),
-        [smem()] + hbm(2) + vmem(1),
-        [
-            pltpu.VMEM((ROWS, 2048), BF16),
-            pltpu.VMEM((ROWS, MODEL), BF16),
-            pltpu.VMEM((8, 128, MODEL), BF16),
-            pltpu.SemaphoreType.DMA((6,)),
-        ],
+        [smem()] + vmem(3),
+        [pltpu.VMEM((8, 128, MODEL), BF16), pltpu.SemaphoreType.DMA((4,))],
         3,
         14,
         out_specs=hbm(1),
-    )(core, *in_hbm(mixed, grad_t), got)[0]
+    )(core, mixed, grad_t, got)[0]
     grad_w = lax.psum_scatter(
         partial, "tm", scatter_dimension=0, axis_index_groups=along_z, tiled=False
     )
@@ -520,14 +507,14 @@
     back = call(
         temporal_backward_kernel,
         shape(ROWS * SENT, 128),
-        [smem()] + hbm(7) + vmem(1) + [smem()],
+        [smem()] + hbm(6) + [pl.BlockSpec(memory_space=pl.ANY)] + vmem(1) + [smem()],
         [wide, pltpu.VMEM((16, 2, 4, 16, MODEL), BF16), pltpu.VMEM((ROWS, 2048), BF16)]
         + [pltpu.VMEM(dims, dtype) for dims, dtype in zip(kept[:5], types)]
         + scan_scratch()
         + [pltpu.SemaphoreType.DMA((37,))],
         7,
         24,
-    )(core, *in_hbm(x_t, mixed, grad_t, bc_t, raw_t, mine, theirs), decay_rate, gain)
+    )(core, *in_hbm(x_t, mixed, grad_t, bc_t, raw_t, mine), theirs, decay_rate, gain)
     back = exchange(back)
 
     mixed_out, grad_x, grad_bc, grad_step = call(

time: 150 us -> 148 us (0.987)
  transfers between devices with their start and end apart: 11 -> 11, of which waited for: 5 -> 6; matrix products, arithmetic and copies ran while one was open for 3% -> 3% of each run, Pallas kernels for 18% -> 18%
where the time goes in v3:
time: 148 us; the launch traced here: 147 us
  blocking collectives  48.1 us (32%)
  waiting for transfers between devices  29.9 us (20%)
  Pallas kernels  26.3 us (18%)
  starting transfers between devices  21 us (14%)
  between operations  14.2 us (10%)
  other arithmetic  5.75 us (4%)
  local copies, waits for them, and re-layouts  2.31 us (2%)
    all_to_all x1, blocking collectives, exchange(): return lax.all_to_all(blocks, 'tm', 0, 0, tiled=True).reshape(v.shape)  48.1 us
    all_to_all x1, waiting for transfers between devices, exchange(): return lax.all_to_all(blocks, 'tm', 0, 0, tiled=True).reshape(v.shape)  19.7 us
    all_to_all x1, starting transfers between devices, weight_part(): return lax.all_to_all(jnp.tile(mine, (8, 1, 1)), 'tm', 0, 0, tiled=True)  9.98 us
    pallas_call x1, Pallas kernels, on_device(): call(temporal_backward_kernel, shape(ROWS * SENT, 128), [smem()] + hbm(6)...  8.4 us
    ppermute x6, starting transfers between devices, gather_weight(): got.append(lax.ppermute(part, ('clip', 'tm'), to))  6.68 us
    pallas_call x1, Pallas kernels, on_device(): call(spatial_backward_kernel, (shape(ROWS, MODEL), shape(ROWS, 2048), sha...  5.47 us
    pallas_call x1, Pallas kernels, on_device(): call(temporal_forward_kernel, tuple((pltpu.HBM(dims, dtype) for dims, dty...  5.02 us
    ppermute x6, waiting for transfers between devices, gather_weight(): got.append(lax.ppermute(part, ('clip', 'tm'), to))  4.99 us
  transfers between devices with their start and end apart: 11, of which 6 were waited for; matrix products, arithmetic and copies ran while one was open for 3% of the time, Pallas kernels for 18%

profile of v3, /device:TPU:1, one launch (start us, length us, event | category | flops | bytes accessed | tf_op | source)
XLA Modules:
  0.0 147.5 jit_solution(18118466994991649845)
XLA Ops:
  7.2 0.9 copy-done
  8.1 0.7 tile.4
  8.8 10.0 %all-to-all-start.1 = ((bf16[16,16,256]{2,1,0:T(8,128)(2,1)}), bf16[16,16,256]{2,1,0:T(8,128)(2,1)S(1)}, u32[]{:S(2)}, u32[]{:S(2)}) async-start(bf16[16,16,256]{2,1,0:T(8,128)(2,1)} %bitcast.12), calls=%async_computation.1 | async-start | bytes 262144 | tf_op jit(solution)/shard_map/all_to_all | solution.py:434
  18.8 0.7 copy-done.4
  19.5 4.9 %shard_map.110.token = bf16[4992,128]{1,0:T(8,128)(2,1)} custom-call(bf16[192,2048]{1,0:T(8,128)(2,1)} %bitcast.38, bf16[192,256]{1,0:T(8,128)(2,1)} %bitcast.40, bf16[64,192]{1,0:T(8,128)(2,1)} %bitcast.42, bf16[192,1024]{1,0:T(8,128)(2,1)} %bitcast.51, f32[2,32]{1,0:T(2,128)S(1)} %copy-done.4), custom_call_target="tpu_custom_call" | custom-call | flops 4000000000 | bytes 12000000 | tf_op jit(solution)/shard_map/pallas_call | solution.py:460
  24.4 3.6 %all-to-all-done.1.v_in = bf16[16,16,256]{2,1,0:T(8,128)(2,1)S(1)} async-done(((bf16[16,16,256]{2,1,0:T(8,128)(2,1)}), bf16[16,16,256]{2,1,0:T(8,128)(2,1)S(1)}, u32[]{:S(2)}, u32[]{:S(2)}) %all-to-all-start.1) | async-done | bytes 131104 | tf_op jit(solution)/shard_map/all_to_all | solution.py:434
  27.9 3.7 %all-to-all-start = ((bf16[16,312,128]{2,1,0:T(8,128)(2,1)}), bf16[16,312,128]{2,1,0:T(8,128)(2,1)S(1)}, u32[]{:S(2)}, u32[]{:S(2)}) async-start(bf16[16,312,128]{2,1,0:T(8,128)(2,1)} %bitcast.8), calls=%async_computation | async-start | bytes 2555904 | tf_op jit(solution)/shard_map/all_to_all | solution.py:384
  31.7 2.6 %collective-permute-start.3 = (bf16[16,16,256]{2,1,0:T(8,128)(2,1)}, bf16[16,16,256]{2,1,0:T(8,128)(2,1)S(1)}, u32[]{:S(2)}, u32[]{:S(2)}) collective-permute-start(bf16[16,16,256]{2,1,0:T(8,128)(2,1)} %shard_map.114), channel_id=1, source_target_pairs={{0,48},{1,193},{2,50},{3,195},{4,52},{5,197},{6,54},{7,199},{8,56}... | collective-permute-start | bytes 393224 | tf_op jit(solution)/shard_map/ppermute | solution.py:445
  34.3 0.5 collective-permute-start.2
  35.1 2.8 %collective-permute-done.3 = bf16[16,16,256]{2,1,0:T(8,128)(2,1)S(1)} collective-permute-done((bf16[16,16,256]{2,1,0:T(8,128)(2,1)}, bf16[16,16,256]{2,1,0:T(8,128)(2,1)S(1)}, u32[]{:S(2)}, u32[]{:S(2)}) %collective-permute-start.3) | collective-permute-done | bytes 131104 | tf_op jit(solution)/shard_map/ppermute | solution.py:445
  38.0 2.2 %collective-permute-done.2 = bf16[16,16,256]{2,1,0:T(8,128)(2,1)S(1)} collective-permute-done((bf16[16,16,256]{2,1,0:T(8,128)(2,1)}, bf16[16,16,256]{2,1,0:T(8,128)(2,1)S(1)}, u32[]{:S(2)}, u32[]{:S(2)}) %collective-permute-start.2) | collective-permute-done | bytes 131104 | tf_op jit(solution)/shard_map/ppermute | solution.py:445
  40.1 1.0 fusion
  41.1 2.5 %collective-permute-start.6 = (bf16[4,16,16,256]{3,2,1,0:T(8,128)(2,1)S(1)}, bf16[4,16,16,256]{3,2,1,0:T(8,128)(2,1)S(1)}, u32[]{:S(2)}, u32[]{:S(2)}) collective-permute-start(bf16[4,16,16,256]{3,2,1,0:T(8,128)(2,1)S(1)} %get-tuple-element.26), channel_id=1, source_target_pairs={{0,192},{1,49},{2,194},{3,51},{4,196},{5,53},{6,198},{7,55},{8,200... | collective-permute-start | bytes 1572872 | tf_op jit(solution)/shard_map/ppermute | solution.py:445
  44.5 19.7 %all-to-all-done = bf16[16,312,128]{2,1,0:T(8,128)(2,1)S(1)} async-done(((bf16[16,312,128]{2,1,0:T(8,128)(2,1)}), bf16[16,312,128]{2,1,0:T(8,128)(2,1)S(1)}, u32[]{:S(2)}, u32[]{:S(2)}) %all-to-all-start) | async-done | bytes 1277984 | tf_op jit(solution)/shard_map/all_to_all | solution.py:384
  64.2 5.0 %shard_map.111 = (bf16[192,2048]{1,0:T(8,128)(2,1)}, bf16[192,2048]{1,0:T(8,128)(2,1)}, bf16[192,1024]{1,0:T(8,128)(2,1)}, bf16[192,128]{1,0:T(8,128)(2,1)}, f32...) custom-call(s32[3]{0:T(128)S(1)} %pad_add_fusion.core_ref.place_ref, bf16[4992,128]{1,0:T(8,128)(2,1)S(1)} %bitcast.35, ...), custom_call_target="tpu_custom_call" | custom-call | flops 4000000000 | bytes 12000000 | tf_op jit(solution)/shard_map/pallas_call | solution.py:480
  69.4 2.9 %pad_maximum_fusion.mine_hbm = bf16[4,4,16,16,256]{4,3,2,1,0:T(8,128)(2,1)} fusion(bf16[1,4,16,16,256]{4,3,2,1,0:T(8,128)(2,1)S(1)} %bitcast.47, bf16[1,4,16,16,256]{4,3,2,1,0:T(8,128)(2,1)} %bitcast.19, bf16[1,4,16,16,256]{4,3,2,1,0:T(8,128)(2,1)} %bitcast.18, bf16[1,4,16,16,256]{4,3,2,1,0:T(8,128)(2,1)S(1)} %get-tuple-element.25), kind=kLoop, calls=%fused_computation | loop fusion | flops 3145728 | bytes 4194304 | tf_op jit(solution)/shard_map/stack | solution.py:446
  72.3 0.5 collective-permute-start.7
  72.7 0.9 collective-permute-done.got_ref
  73.7 2.4 %shard_map.112.token = bf16[8,128,1024]{2,1,0:T(8,128)(2,1)} custom-call(s32[3]{0:T(128)S(1)} %pad_add_fusion.core_ref.place_ref, bf16[192,2048]{1,0:T(8,128)(2,1)S(1)} %copy-done.7, bf16[192,1024]{1,0:T(8,128)(2,1)S(1)} %copy-done.8, bf16[8,128,1024]{2,1,0:T(8,128)(2,1)S(1)} %collective-permute-done.got_ref), custom_call_target="tpu_custom_call" | custom-call | flops 3000000000 | bytes 9000000 | tf_op jit(solution)/shard_map/pallas_call | solution.py:493
  76.2 0.7 collective-permute-done.7.theirs_hbm
  76.9 8.4 %shard_map.115 = bf16[4992,128]{1,0:T(8,128)(2,1)S(1)} custom-call(s32[3]{0:T(128)S(1)} %pad_add_fusion.core_ref.place_ref, bf16[192,2048]{1,0:T(8,128)(2,1)} %get-tuple-element.15.x_hbm, bf16[192,2048]{1,0:T(8,128)(2,1)} %get-tuple-element.16.mixed_ref.mixed_hbm, bf16[192,1024]{1,0:T(8,128)(2,1)} %get-tuple-element.17.grad_ref.grad_hbm, ...), custom_call_target="tpu_custom_call" | custom-call | flops 7000000000 | bytes 21000000 | tf_op jit(solution)/shard_map/pallas_call | solution.py:507
  85.3 48.1 %all_to_all.15 = bf16[16,312,128]{2,1,0:T(8,128)(2,1)S(1)} all-to-all(bf16[16,312,128]{2,1,0:T(8,128)(2,1)S(1)} %bitcast.36), channel_id=1, replica_groups=mesh['clip'=16,'tm'=16] {'tm'}, dimensions={0} | all-to-all | bytes 2555904 | tf_op jit(solution)/shard_map/all_to_all | solution.py:384
  133.4 5.5 %shard_map.116 = (bf16[192,1024]{1,0:T(8,128)(2,1)}, bf16[192,2048]{1,0:T(8,128)(2,1)}, bf16[192,256]{1,0:T(8,128)(2,1)}, bf16[64,192]{1,0:T(8,128)(2,1)}) custom-call(bf16[192,2048]{1,0:T(8,128)(2,1)S(1)} %bitcast.39, bf16[4992,128]{1,0:T(8,128)(2,1)S(1)} %bitcast.37, bf16[192,256]{1,0:T(8,128)(2,1)S(1)} %bitcast.41, bf16[64,192]{1,0:T(8,128)(2,1)S(1)} %bitcast.43, ...), custom_call_target="tpu_custom_call" | custom-call | flops 8000000000 | bytes 24000000 | tf_op jit(solution)/shard_map/pallas_call | solution.py:520
  138.8 1.8 %bitcast_convert_fusion = f32[128,1024]{1,0:T(8,128)} fusion(bf16[1,128,1024]{2,1,0:T(8,128)(2,1)} %reduce-scatter.2.cloned.1.call-done), kind=kLoop, calls=%fused_computation.2 | loop fusion | flops 131072 | bytes 786432 | tf_op jit(solution)/shard_map/convert_element_type | solution.py:528
  (33 shorter events, 1.4 us)
Async XLA Ops:
  7.2 1.0 copy-start
  8.8 19.1 %all-to-all-start.1 = ((bf16[16,16,256]{2,1,0:T(8,128)(2,1)}), bf16[16,16,256]{2,1,0:T(8,128)(2,1)S(1)}, u32[]{:S(2)}, u32[]{:S(2)}) async-start(bf16[16,16,256]{2,1,0:T(8,128)(2,1)} %bitcast.12), calls=%async_computation.1 | async-start | bytes 262144 | tf_op jit(solution)/shard_map/all_to_all | solution.py:434
  18.8 0.7 copy-start.4
  27.9 3.8 %copy-start.9 = (bf16[16,16,256]{2,1,0:T(8,128)(2,1)}, bf16[16,16,256]{2,1,0:T(8,128)(2,1)S(1)}, u32[]{:S(2)}) copy-start(bf16[16,16,256]{2,1,0:T(8,128)(2,1)S(1)} %all-to-all-done.1.v_in) | copy-start | bytes 393220
  27.9 36.2 %all-to-all-start = ((bf16[16,312,128]{2,1,0:T(8,128)(2,1)}), bf16[16,312,128]{2,1,0:T(8,128)(2,1)S(1)}, u32[]{:S(2)}, u32[]{:S(2)}) async-start(bf16[16,312,128]{2,1,0:T(8,128)(2,1)} %bitcast.8), calls=%async_computation | async-start | bytes 2555904 | tf_op jit(solution)/shard_map/all_to_all | solution.py:384
  31.6 32.5 %copy-start.5 = (f32[2,32]{1,0:T(2,128)S(1)}, f32[2,32]{1,0:T(2,128)}, u32[]{:S(2)}) copy-start(f32[2,32]{1,0:T(2,128)} %rate_ref.7) | copy-start | bytes 772
  31.6 32.5 %copy-start.6 = (f32[32]{0:T(128)S(1)}, f32[32]{0:T(128)}, u32[]{:S(2)}) copy-start(f32[32]{0:T(128)} %param.11) | copy-start | bytes 388
  31.7 107.2 %reduce-scatter.2.cloned.1.call-start = ((), (), s32[]{:S(2)}) async-start(), calls=%async_computation.4 | async-start | bytes 2359296 | tf_op jit(solution)/shard_map/reduce_scatter | solution.py:502
  31.7 6.2 %collective-permute-start.3 = (bf16[16,16,256]{2,1,0:T(8,128)(2,1)}, bf16[16,16,256]{2,1,0:T(8,128)(2,1)S(1)}, u32[]{:S(2)}, u32[]{:S(2)}) collective-permute-start(bf16[16,16,256]{2,1,0:T(8,128)(2,1)} %shard_map.114), channel_id=1, source_target_pairs={{0,48},{1,193},{2,50},{3,195},{4,52},{5,197},{6,54},{7,199},{8,56}... | collective-permute-start | bytes 393224 | tf_op jit(solution)/shard_map/ppermute | solution.py:445
  34.3 5.8 %collective-permute-start.2 = (bf16[16,16,256]{2,1,0:T(8,128)(2,1)}, bf16[16,16,256]{2,1,0:T(8,128)(2,1)S(1)}, u32[]{:S(2)}, u32[]{:S(2)}) collective-permute-start(bf16[16,16,256]{2,1,0:T(8,128)(2,1)} %shard_map.114), channel_id=1, source_target_pairs={{0,32},{1,129},{2,34},{3,131},{4,36},{5,133},{6,38},{7,135},{8,40}... | collective-permute-start | bytes 393224 | tf_op jit(solution)/shard_map/ppermute | solution.py:445
  34.8 5.3 %collective-permute-start.1 = (bf16[16,16,256]{2,1,0:T(8,128)(2,1)}, bf16[16,16,256]{2,1,0:T(8,128)(2,1)S(1)}, u32[]{:S(2)}, u32[]{:S(2)}) collective-permute-start(bf16[16,16,256]{2,1,0:T(8,128)(2,1)} %shard_map.114), channel_id=1, source_target_pairs={{0,16},{1,65},{2,18},{3,67},{4,20},{5,69},{6,22},{7,71},{8,24},{9,... | collective-permute-start | bytes 393224 | tf_op jit(solution)/shard_map/ppermute | solution.py:445
  41.1 28.2 %collective-permute-start.6 = (bf16[4,16,16,256]{3,2,1,0:T(8,128)(2,1)S(1)}, bf16[4,16,16,256]{3,2,1,0:T(8,128)(2,1)S(1)}, u32[]{:S(2)}, u32[]{:S(2)}) collective-permute-start(bf16[4,16,16,256]{3,2,1,0:T(8,128)(2,1)S(1)} %get-tuple-element.26), channel_id=1, source_target_pairs={{0,192},{1,49},{2,194},{3,51},{4,196},{5,53},{6,198},{7,55},{8,200... | collective-permute-start | bytes 1572872 | tf_op jit(solution)/shard_map/ppermute | solution.py:445
  43.6 25.7 %collective-permute-start.5 = (bf16[4,16,16,256]{3,2,1,0:T(8,128)(2,1)S(1)}, bf16[4,16,16,256]{3,2,1,0:T(8,128)(2,1)}, u32[]{:S(2)}, u32[]{:S(2)}) collective-permute-start(bf16[4,16,16,256]{3,2,1,0:T(8,128)(2,1)S(1)} %get-tuple-element.26), channel_id=1, source_target_pairs={{0,128},{1,33},{2,130},{3,35},{4,132},{5,37},{6,134},{7,39},{8,136... | collective-permute-start | bytes 1572872 | tf_op jit(solution)/shard_map/ppermute | solution.py:445
  44.0 25.3 %collective-permute-start.4 = (bf16[4,16,16,256]{3,2,1,0:T(8,128)(2,1)S(1)}, bf16[4,16,16,256]{3,2,1,0:T(8,128)(2,1)}, u32[]{:S(2)}, u32[]{:S(2)}) collective-permute-start(bf16[4,16,16,256]{3,2,1,0:T(8,128)(2,1)S(1)} %get-tuple-element.26), channel_id=1, source_target_pairs={{0,64},{1,17},{2,66},{3,19},{4,68},{5,21},{6,70},{7,23},{8,72},{9,... | collective-permute-start | bytes 1572872 | tf_op jit(solution)/shard_map/ppermute | solution.py:445
  69.2 4.5 %collective-permute-start = (bf16[8,128,1024]{2,1,0:T(8,128)(2,1)}, bf16[8,128,1024]{2,1,0:T(8,128)(2,1)S(1)}, u32[]{:S(2)}, u32[]{:S(2)}) collective-permute-start(bf16[8,128,1024]{2,1,0:T(8,128)(2,1)} %get-tuple-element.20), channel_id=1, source_target_pairs={{0,1},{1,0},{2,3},{3,2},{4,5},{5,4},{6,7},{7,6},{8,9},{9,8},{10,11... | collective-permute-start | bytes 6291464 | tf_op jit(solution)/shard_map/ppermute | solution.py:408
  69.3 4.3 %copy-start.7 = (bf16[192,2048]{1,0:T(8,128)(2,1)S(1)}, bf16[192,2048]{1,0:T(8,128)(2,1)}, u32[]{:S(2)}) copy-start(bf16[192,2048]{1,0:T(8,128)(2,1)} %get-tuple-element.16.mixed_ref.mixed_hbm) | copy-start | bytes 2359300
  69.4 4.3 %copy-start.8 = (bf16[192,1024]{1,0:T(8,128)(2,1)S(1)}, bf16[192,1024]{1,0:T(8,128)(2,1)}, u32[]{:S(2)}) copy-start(bf16[192,1024]{1,0:T(8,128)(2,1)} %get-tuple-element.17.grad_ref.grad_hbm) | copy-start | bytes 1179652
  72.3 4.6 %collective-permute-start.7 = (bf16[4,4,16,16,256]{4,3,2,1,0:T(8,128)(2,1)}, bf16[4,4,16,16,256]{4,3,2,1,0:T(8,128)(2,1)}, u32[]{:S(2)}, u32[]{:S(2)}) collective-permute-start(bf16[4,4,16,16,256]{4,3,2,1,0:T(8,128)(2,1)} %pad_maximum_fusion.mine_hbm), channel_id=1, source_target_pairs={{0,1},{1,0},{2,3},{3,2},{4,5},{5,4},{6,7},{7,6},{8,9},{9,8},{10,11... | collective-permute-start | bytes 6291464 | tf_op jit(solution)/shard_map/ppermute | solution.py:408
  85.3 48.1 %copy-start.1 = (bf16[1,192,2048]{2,1,0:T(8,128)(2,1)S(1)}, bf16[1,192,2048]{2,1,0:T(8,128)(2,1)}, u32[]{:S(2)}) copy-start(bf16[1,192,2048]{2,1,0:T(8,128)(2,1)} %param.7) | copy-start | bytes 2359300
  85.3 48.1 %copy-start.2 = (bf16[1,192,256]{2,1,0:T(8,128)(2,1)S(1)}, bf16[1,192,256]{2,1,0:T(8,128)(2,1)}, u32[]{:S(2)}) copy-start(bf16[1,192,256]{2,1,0:T(8,128)(2,1)} %param.8) | copy-start | bytes 294916
  85.3 48.1 %copy-start.3 = (bf16[1,192,64]{1,2,0:T(8,128)(2,1)S(1)}, bf16[1,192,64]{1,2,0:T(8,128)(2,1)}, u32[]{:S(2)}) copy-start(bf16[1,192,64]{1,2,0:T(8,128)(2,1)} %param.9) | copy-start | bytes 73732
Sparse Core Ops, SparseCore 0:
  76.3 60.5 reduce-scatter.1

commit v4 on v3

--- a/solution.py
+++ b/solution.py
@@ -507,14 +507,14 @@
     back = call(
         temporal_backward_kernel,
         shape(ROWS * SENT, 128),
-        [smem()] + hbm(6) + [pl.BlockSpec(memory_space=pl.ANY)] + vmem(1) + [smem()],
+        [smem()] + hbm(5) + [pl.BlockSpec(memory_space=pl.ANY)] * 2 + vmem(1) + [smem()],
         [wide, pltpu.VMEM((16, 2, 4, 16, MODEL), BF16), pltpu.VMEM((ROWS, 2048), BF16)]
         + [pltpu.VMEM(dims, dtype) for dims, dtype in zip(kept[:5], types)]
         + scan_scratch()
         + [pltpu.SemaphoreType.DMA((37,))],
         7,
         24,
-    )(core, *in_hbm(x_t, mixed, grad_t, bc_t, raw_t, mine), theirs, decay_rate, gain)
+    )(core, *in_hbm(x_t, mixed, grad_t, bc_t, raw_t), mine, theirs, decay_rate, gain)
     back = exchange(back)
 
     mixed_out, grad_x, grad_bc, grad_step = call(

time: 148 us -> 148 us (level)
  transfers between devices with their start and end apart: 11 -> 11, of which waited for: 6 -> 6; matrix products, arithmetic and copies ran while one was open for 3% -> 2% of each run, Pallas kernels for 18% -> 17%
where the time goes in v4:
time: 148 us
  blocking collectives  49 us (33%)
  waiting for transfers between devices  30.1 us (20%)
  Pallas kernels  25.7 us (17%)
  starting transfers between devices  21.1 us (14%)
  between operations  14.2 us (10%)
  other arithmetic  5.05 us (3%)
  local copies, waits for them, and re-layouts  2.31 us (2%)
    all_to_all x1, blocking collectives, exchange(): return lax.all_to_all(blocks, 'tm', 0, 0, tiled=True).reshape(v.shape)  49 us
    all_to_all x1, waiting for transfers between devices, exchange(): return lax.all_to_all(blocks, 'tm', 0, 0, tiled=True).reshape(v.shape)  19 us
    all_to_all x1, starting transfers between devices, weight_part(): return lax.all_to_all(jnp.tile(mine, (8, 1, 1)), 'tm', 0, 0, tiled=True)  9.98 us
    pallas_call x1, Pallas kernels, on_device(): call(temporal_backward_kernel, shape(ROWS * SENT, 128), [smem()] + hbm(5)...  7.82 us
    ppermute x6, starting transfers between devices, gather_weight(): got.append(lax.ppermute(part, ('clip', 'tm'), to))  6.59 us
    pallas_call x1, Pallas kernels, on_device(): call(spatial_backward_kernel, (shape(ROWS, MODEL), shape(ROWS, 2048), sha...  5.47 us
    pallas_call x1, Pallas kernels, on_device(): call(temporal_forward_kernel, tuple((pltpu.HBM(dims, dtype) for dims, dty...  5.02 us
    ppermute x6, waiting for transfers between devices, gather_weight(): got.append(lax.ppermute(part, ('clip', 'tm'), to))  4.99 us
  transfers between devices with their start and end apart: 11, of which 6 were waited for; matrix products, arithmetic and copies ran while one was open for 2% of the time, Pallas kernels for 17%

profile of v4, /device:TPU:1, one launch (start us, length us, event | category | flops | bytes accessed | tf_op | source)
XLA Modules:
  0.0 147.6 jit_solution(9509042680189225464)
XLA Ops:
  7.2 0.9 copy-done
  8.1 0.7 tile.4
  8.8 10.0 %all-to-all-start.1 = ((bf16[16,16,256]{2,1,0:T(8,128)(2,1)}), bf16[16,16,256]{2,1,0:T(8,128)(2,1)S(1)}, u32[]{:S(2)}, u32[]{:S(2)}) async-start(bf16[16,16,256]{2,1,0:T(8,128)(2,1)} %bitcast.12), calls=%async_computation.1 | async-start | bytes 262144 | tf_op jit(solution)/shard_map/all_to_all | solution.py:434
  18.8 0.7 copy-done.4
  19.5 4.9 %shard_map.110.token = bf16[4992,128]{1,0:T(8,128)(2,1)} custom-call(bf16[192,2048]{1,0:T(8,128)(2,1)} %bitcast.38, bf16[192,256]{1,0:T(8,128)(2,1)} %bitcast.40, bf16[64,192]{1,0:T(8,128)(2,1)} %bitcast.42, bf16[192,1024]{1,0:T(8,128)(2,1)} %bitcast.52, f32[2,32]{1,0:T(2,128)S(1)} %copy-done.4), custom_call_target="tpu_custom_call" | custom-call | flops 4000000000 | bytes 12000000 | tf_op jit(solution)/shard_map/pallas_call | solution.py:460
  24.4 3.6 %all-to-all-done.1.v_in = bf16[16,16,256]{2,1,0:T(8,128)(2,1)S(1)} async-done(((bf16[16,16,256]{2,1,0:T(8,128)(2,1)}), bf16[16,16,256]{2,1,0:T(8,128)(2,1)S(1)}, u32[]{:S(2)}, u32[]{:S(2)}) %all-to-all-start.1) | async-done | bytes 131104 | tf_op jit(solution)/shard_map/all_to_all | solution.py:434
  27.9 3.7 %all-to-all-start = ((bf16[16,312,128]{2,1,0:T(8,128)(2,1)}), bf16[16,312,128]{2,1,0:T(8,128)(2,1)S(1)}, u32[]{:S(2)}, u32[]{:S(2)}) async-start(bf16[16,312,128]{2,1,0:T(8,128)(2,1)} %bitcast.8), calls=%async_computation | async-start | bytes 2555904 | tf_op jit(solution)/shard_map/all_to_all | solution.py:384
  31.7 2.6 %collective-permute-start.3 = (bf16[16,16,256]{2,1,0:T(8,128)(2,1)}, bf16[16,16,256]{2,1,0:T(8,128)(2,1)S(1)}, u32[]{:S(2)}, u32[]{:S(2)}) collective-permute-start(bf16[16,16,256]{2,1,0:T(8,128)(2,1)} %shard_map.114), channel_id=1, source_target_pairs={{0,48},{1,193},{2,50},{3,195},{4,52},{5,197},{6,54},{7,199},{8,56}... | collective-permute-start | bytes 393224 | tf_op jit(solution)/shard_map/ppermute | solution.py:445
  34.3 0.5 collective-permute-start.2
  35.1 2.8 %collective-permute-done.3 = bf16[16,16,256]{2,1,0:T(8,128)(2,1)S(1)} collective-permute-done((bf16[16,16,256]{2,1,0:T(8,128)(2,1)}, bf16[16,16,256]{2,1,0:T(8,128)(2,1)S(1)}, u32[]{:S(2)}, u32[]{:S(2)}) %collective-permute-start.3) | collective-permute-done | bytes 131104 | tf_op jit(solution)/shard_map/ppermute | solution.py:445
  38.0 2.2 %collective-permute-done.2 = bf16[16,16,256]{2,1,0:T(8,128)(2,1)S(1)} collective-permute-done((bf16[16,16,256]{2,1,0:T(8,128)(2,1)}, bf16[16,16,256]{2,1,0:T(8,128)(2,1)S(1)}, u32[]{:S(2)}, u32[]{:S(2)}) %collective-permute-start.2) | collective-permute-done | bytes 131104 | tf_op jit(solution)/shard_map/ppermute | solution.py:445
  40.1 1.8 %fusion = (bf16[1,4,16,16,256]{4,3,2,1,0:T(8,128)(2,1)}, bf16[4,16,16,256]{3,2,1,0:T(8,128)(2,1)S(1)}) fusion(bf16[1,16,16,256]{3,2,1,0:T(8,128)(2,1)S(1)} %bitcast.49, bf16[1,16,16,256]{3,2,1,0:T(8,128)(2,1)S(1)} %bitcast.50, bf16[1,16,16,256]{3,2,1,0:T(8,128)(2,1)S(1)} %bitcast.51, bf16[1,16,16,256]{3,2,1,0:T(8,128)(2,1)} %bitcast.46), kind=kLoop, calls=%fused_computation.5 | loop fusion | flops 786432 | bytes 1572864 | tf_op jit(solution)/shard_map/stack | solution.py:446
  41.9 2.4 %collective-permute-start.6 = (bf16[4,16,16,256]{3,2,1,0:T(8,128)(2,1)S(1)}, bf16[4,16,16,256]{3,2,1,0:T(8,128)(2,1)S(1)}, u32[]{:S(2)}, u32[]{:S(2)}) collective-permute-start(bf16[4,16,16,256]{3,2,1,0:T(8,128)(2,1)S(1)} %get-tuple-element.26), channel_id=1, source_target_pairs={{0,192},{1,49},{2,194},{3,51},{4,196},{5,53},{6,198},{7,55},{8,200... | collective-permute-start | bytes 1572872 | tf_op jit(solution)/shard_map/ppermute | solution.py:445
  44.7 0.5 collective-permute-start.4
  45.2 19.0 %all-to-all-done = bf16[16,312,128]{2,1,0:T(8,128)(2,1)S(1)} async-done(((bf16[16,312,128]{2,1,0:T(8,128)(2,1)}), bf16[16,312,128]{2,1,0:T(8,128)(2,1)S(1)}, u32[]{:S(2)}, u32[]{:S(2)}) %all-to-all-start) | async-done | bytes 1277984 | tf_op jit(solution)/shard_map/all_to_all | solution.py:384
  64.2 5.0 %shard_map.111 = (bf16[192,2048]{1,0:T(8,128)(2,1)}, bf16[192,2048]{1,0:T(8,128)(2,1)}, bf16[192,1024]{1,0:T(8,128)(2,1)}, bf16[192,128]{1,0:T(8,128)(2,1)}, f32...) custom-call(s32[3]{0:T(128)S(1)} %pad_add_fusion.core_ref.place_ref, bf16[4992,128]{1,0:T(8,128)(2,1)S(1)} %bitcast.35, ...), custom_call_target="tpu_custom_call" | custom-call | flops 4000000000 | bytes 12000000 | tf_op jit(solution)/shard_map/pallas_call | solution.py:480
  69.4 1.4 pad_maximum_fusion.mine_hbm
  70.8 0.7 collective-permute-start.7
  71.5 2.1 %collective-permute-done.got_ref = bf16[8,128,1024]{2,1,0:T(8,128)(2,1)S(1)} collective-permute-done((bf16[8,128,1024]{2,1,0:T(8,128)(2,1)}, bf16[8,128,1024]{2,1,0:T(8,128)(2,1)S(1)}, u32[]{:S(2)}, u32[]{:S(2)}) %collective-permute-start) | collective-permute-done | bytes 2097184 | tf_op jit(solution)/shard_map/ppermute | solution.py:408
  73.7 2.5 %shard_map.112.token = bf16[8,128,1024]{2,1,0:T(8,128)(2,1)} custom-call(s32[3]{0:T(128)S(1)} %pad_add_fusion.core_ref.place_ref, bf16[192,2048]{1,0:T(8,128)(2,1)S(1)} %copy-done.7, bf16[192,1024]{1,0:T(8,128)(2,1)S(1)} %copy-done.8, bf16[8,128,1024]{2,1,0:T(8,128)(2,1)S(1)} %collective-permute-done.got_ref), custom_call_target="tpu_custom_call" | custom-call | flops 3000000000 | bytes 9000000 | tf_op jit(solution)/shard_map/pallas_call | solution.py:493
  76.6 7.8 %shard_map.115 = bf16[4992,128]{1,0:T(8,128)(2,1)S(1)} custom-call(s32[3]{0:T(128)S(1)} %pad_add_fusion.core_ref.place_ref, bf16[192,2048]{1,0:T(8,128)(2,1)} %get-tuple-element.15.x_hbm, bf16[192,2048]{1,0:T(8,128)(2,1)} %get-tuple-element.16.mixed_ref.mixed_hbm, bf16[192,1024]{1,0:T(8,128)(2,1)} %get-tuple-element.17.grad_ref.grad_hbm, ...), custom_call_target="tpu_custom_call" | custom-call | flops 7000000000 | bytes 21000000 | tf_op jit(solution)/shard_map/pallas_call | solution.py:507
  84.5 49.0 %all_to_all.15 = bf16[16,312,128]{2,1,0:T(8,128)(2,1)S(1)} all-to-all(bf16[16,312,128]{2,1,0:T(8,128)(2,1)S(1)} %bitcast.36), channel_id=1, replica_groups=mesh['clip'=16,'tm'=16] {'tm'}, dimensions={0} | all-to-all | bytes 2555904 | tf_op jit(solution)/shard_map/all_to_all | solution.py:384
  133.4 5.5 %shard_map.116 = (bf16[192,1024]{1,0:T(8,128)(2,1)}, bf16[192,2048]{1,0:T(8,128)(2,1)}, bf16[192,256]{1,0:T(8,128)(2,1)}, bf16[64,192]{1,0:T(8,128)(2,1)}) custom-call(bf16[192,2048]{1,0:T(8,128)(2,1)S(1)} %bitcast.39, bf16[4992,128]{1,0:T(8,128)(2,1)S(1)} %bitcast.37, bf16[192,256]{1,0:T(8,128)(2,1)S(1)} %bitcast.41, bf16[64,192]{1,0:T(8,128)(2,1)S(1)} %bitcast.43, ...), custom_call_target="tpu_custom_call" | custom-call | flops 8000000000 | bytes 24000000 | tf_op jit(solution)/shard_map/pallas_call | solution.py:520
  138.9 1.8 %bitcast_convert_fusion = f32[128,1024]{1,0:T(8,128)} fusion(bf16[1,128,1024]{2,1,0:T(8,128)(2,1)} %reduce-scatter.2.cloned.1.call-done), kind=kLoop, calls=%fused_computation.2 | loop fusion | flops 131072 | bytes 786432 | tf_op jit(solution)/shard_map/convert_element_type | solution.py:528
  (35 shorter events, 1.3 us)
Async XLA Ops:
  7.2 1.0 copy-start
  8.8 19.1 %all-to-all-start.1 = ((bf16[16,16,256]{2,1,0:T(8,128)(2,1)}), bf16[16,16,256]{2,1,0:T(8,128)(2,1)S(1)}, u32[]{:S(2)}, u32[]{:S(2)}) async-start(bf16[16,16,256]{2,1,0:T(8,128)(2,1)} %bitcast.12), calls=%async_computation.1 | async-start | bytes 262144 | tf_op jit(solution)/shard_map/all_to_all | solution.py:434
  18.8 0.7 copy-start.4
  27.9 3.8 %copy-start.10 = (bf16[16,16,256]{2,1,0:T(8,128)(2,1)}, bf16[16,16,256]{2,1,0:T(8,128)(2,1)S(1)}, u32[]{:S(2)}) copy-start(bf16[16,16,256]{2,1,0:T(8,128)(2,1)S(1)} %all-to-all-done.1.v_in) | copy-start | bytes 393220
  27.9 36.2 %all-to-all-start = ((bf16[16,312,128]{2,1,0:T(8,128)(2,1)}), bf16[16,312,128]{2,1,0:T(8,128)(2,1)S(1)}, u32[]{:S(2)}, u32[]{:S(2)}) async-start(bf16[16,312,128]{2,1,0:T(8,128)(2,1)} %bitcast.8), calls=%async_computation | async-start | bytes 2555904 | tf_op jit(solution)/shard_map/all_to_all | solution.py:384
  31.6 32.5 %copy-start.5 = (f32[2,32]{1,0:T(2,128)S(1)}, f32[2,32]{1,0:T(2,128)}, u32[]{:S(2)}) copy-start(f32[2,32]{1,0:T(2,128)} %rate_ref.7) | copy-start | bytes 772
  31.6 32.5 %copy-start.6 = (f32[32]{0:T(128)S(1)}, f32[32]{0:T(128)}, u32[]{:S(2)}) copy-start(f32[32]{0:T(128)} %param.11) | copy-start | bytes 388
  31.7 107.3 %reduce-scatter.2.cloned.1.call-start = ((), (), s32[]{:S(2)}) async-start(), calls=%async_computation.4 | async-start | bytes 2359296 | tf_op jit(solution)/shard_map/reduce_scatter | solution.py:502
  31.7 6.2 %collective-permute-start.3 = (bf16[16,16,256]{2,1,0:T(8,128)(2,1)}, bf16[16,16,256]{2,1,0:T(8,128)(2,1)S(1)}, u32[]{:S(2)}, u32[]{:S(2)}) collective-permute-start(bf16[16,16,256]{2,1,0:T(8,128)(2,1)} %shard_map.114), channel_id=1, source_target_pairs={{0,48},{1,193},{2,50},{3,195},{4,52},{5,197},{6,54},{7,199},{8,56}... | collective-permute-start | bytes 393224 | tf_op jit(solution)/shard_map/ppermute | solution.py:445
  34.3 5.8 %collective-permute-start.2 = (bf16[16,16,256]{2,1,0:T(8,128)(2,1)}, bf16[16,16,256]{2,1,0:T(8,128)(2,1)S(1)}, u32[]{:S(2)}, u32[]{:S(2)}) collective-permute-start(bf16[16,16,256]{2,1,0:T(8,128)(2,1)} %shard_map.114), channel_id=1, source_target_pairs={{0,32},{1,129},{2,34},{3,131},{4,36},{5,133},{6,38},{7,135},{8,40}... | collective-permute-start | bytes 393224 | tf_op jit(solution)/shard_map/ppermute | solution.py:445
  34.8 5.3 %collective-permute-start.1 = (bf16[16,16,256]{2,1,0:T(8,128)(2,1)}, bf16[16,16,256]{2,1,0:T(8,128)(2,1)S(1)}, u32[]{:S(2)}, u32[]{:S(2)}) collective-permute-start(bf16[16,16,256]{2,1,0:T(8,128)(2,1)} %shard_map.114), channel_id=1, source_target_pairs={{0,16},{1,65},{2,18},{3,67},{4,20},{5,69},{6,22},{7,71},{8,24},{9,... | collective-permute-start | bytes 393224 | tf_op jit(solution)/shard_map/ppermute | solution.py:445
  41.9 27.4 %collective-permute-start.6 = (bf16[4,16,16,256]{3,2,1,0:T(8,128)(2,1)S(1)}, bf16[4,16,16,256]{3,2,1,0:T(8,128)(2,1)S(1)}, u32[]{:S(2)}, u32[]{:S(2)}) collective-permute-start(bf16[4,16,16,256]{3,2,1,0:T(8,128)(2,1)S(1)} %get-tuple-element.26), channel_id=1, source_target_pairs={{0,192},{1,49},{2,194},{3,51},{4,196},{5,53},{6,198},{7,55},{8,200... | collective-permute-start | bytes 1572872 | tf_op jit(solution)/shard_map/ppermute | solution.py:445
  44.3 25.0 %collective-permute-start.5 = (bf16[4,16,16,256]{3,2,1,0:T(8,128)(2,1)S(1)}, bf16[4,16,16,256]{3,2,1,0:T(8,128)(2,1)S(1)}, u32[]{:S(2)}, u32[]{:S(2)}) collective-permute-start(bf16[4,16,16,256]{3,2,1,0:T(8,128)(2,1)S(1)} %get-tuple-element.26), channel_id=1, source_target_pairs={{0,128},{1,33},{2,130},{3,35},{4,132},{5,37},{6,134},{7,39},{8,136... | collective-permute-start | bytes 1572872 | tf_op jit(solution)/shard_map/ppermute | solution.py:445
  44.7 24.6 %collective-permute-start.4 = (bf16[4,16,16,256]{3,2,1,0:T(8,128)(2,1)S(1)}, bf16[4,16,16,256]{3,2,1,0:T(8,128)(2,1)}, u32[]{:S(2)}, u32[]{:S(2)}) collective-permute-start(bf16[4,16,16,256]{3,2,1,0:T(8,128)(2,1)S(1)} %get-tuple-element.26), channel_id=1, source_target_pairs={{0,64},{1,17},{2,66},{3,19},{4,68},{5,21},{6,70},{7,23},{8,72},{9,... | collective-permute-start | bytes 1572872 | tf_op jit(solution)/shard_map/ppermute | solution.py:445
  64.2 5.2 %copy-start.9 = (bf16[1,4,16,16,256]{4,3,2,1,0:T(8,128)(2,1)S(1)}, bf16[1,4,16,16,256]{4,3,2,1,0:T(8,128)(2,1)}, u32[]{:S(2)}) copy-start(bf16[1,4,16,16,256]{4,3,2,1,0:T(8,128)(2,1)} %get-tuple-element.25) | copy-start | bytes 1572868
  69.2 4.5 %collective-permute-start = (bf16[8,128,1024]{2,1,0:T(8,128)(2,1)}, bf16[8,128,1024]{2,1,0:T(8,128)(2,1)S(1)}, u32[]{:S(2)}, u32[]{:S(2)}) collective-permute-start(bf16[8,128,1024]{2,1,0:T(8,128)(2,1)} %get-tuple-element.20), channel_id=1, source_target_pairs={{0,1},{1,0},{2,3},{3,2},{4,5},{5,4},{6,7},{7,6},{8,9},{9,8},{10,11... | collective-permute-start | bytes 6291464 | tf_op jit(solution)/shard_map/ppermute | solution.py:408
  69.4 4.3 %copy-start.7 = (bf16[192,2048]{1,0:T(8,128)(2,1)S(1)}, bf16[192,2048]{1,0:T(8,128)(2,1)}, u32[]{:S(2)}) copy-start(bf16[192,2048]{1,0:T(8,128)(2,1)} %get-tuple-element.16.mixed_ref.mixed_hbm) | copy-start | bytes 2359300
  69.4 4.3 %copy-start.8 = (bf16[192,1024]{1,0:T(8,128)(2,1)S(1)}, bf16[192,1024]{1,0:T(8,128)(2,1)}, u32[]{:S(2)}) copy-start(bf16[192,1024]{1,0:T(8,128)(2,1)} %get-tuple-element.17.grad_ref.grad_hbm) | copy-start | bytes 1179652
  70.8 5.8 %collective-permute-start.7 = (bf16[4,4,16,16,256]{4,3,2,1,0:T(8,128)(2,1)S(1)}, bf16[4,4,16,16,256]{4,3,2,1,0:T(8,128)(2,1)}, u32[]{:S(2)}, u32[]{:S(2)}) collective-permute-start(bf16[4,4,16,16,256]{4,3,2,1,0:T(8,128)(2,1)S(1)} %pad_maximum_fusion.mine_hbm), channel_id=1, source_target_pairs={{0,1},{1,0},{2,3},{3,2},{4,5},{5,4},{6,7},{7,6},{8,9},{9,8},{10,11... | collective-permute-start | bytes 6291464 | tf_op jit(solution)/shard_map/ppermute | solution.py:408
  84.4 49.0 %copy-start.1 = (bf16[1,192,2048]{2,1,0:T(8,128)(2,1)S(1)}, bf16[1,192,2048]{2,1,0:T(8,128)(2,1)}, u32[]{:S(2)}) copy-start(bf16[1,192,2048]{2,1,0:T(8,128)(2,1)} %param.7) | copy-start | bytes 2359300
  84.4 49.0 %copy-start.2 = (bf16[1,192,256]{2,1,0:T(8,128)(2,1)S(1)}, bf16[1,192,256]{2,1,0:T(8,128)(2,1)}, u32[]{:S(2)}) copy-start(bf16[1,192,256]{2,1,0:T(8,128)(2,1)} %param.8) | copy-start | bytes 294916
  84.4 49.0 %copy-start.3 = (bf16[1,192,64]{1,2,0:T(8,128)(2,1)S(1)}, bf16[1,192,64]{1,2,0:T(8,128)(2,1)}, u32[]{:S(2)}) copy-start(bf16[1,192,64]{1,2,0:T(8,128)(2,1)} %param.9) | copy-start | bytes 73732
Sparse Core Ops, SparseCore 0:
  76.3 59.8 reduce-scatter.1
